TPU v7x, 32 devices: a whole 2x2x4 slice. The times are simulated.
32 devices in a mesh: col: 4 (over y, x), ta: 8 (over z, core).
Axes of the slice: x: 2, y: 2, z: 4, core: 2. Of those that a mesh axis runs over, the one named last changes fastest.
Arguments:
- frames: bfloat16 [672, 14, 14, 1024], P(('col', 'ta')), may hold values from -6 to 6
- out_grad: bfloat16 [672, 14, 14, 1024], P(('col', 'ta')), may hold values from -6 to 6
- held: int32 [4, 8], replicated, may hold values from 3 to 21, as said below
- clip_stride: int32 [4, 24], replicated, may hold values from 1 to 4, as said below
- w_reduce: bfloat16 [2, 1024, 256], replicated, may hold values from -0.1875 to 0.1875
- w_mid: bfloat16 [2, 256, 256], replicated, may hold values from -0.375 to 0.375
- depth_kernel: bfloat16 [2, 27, 256], replicated, may hold values from -1.25 to 1.25
- w_expand: bfloat16 [2, 256, 1024], replicated, may hold values from -0.375 to 0.375
- narrow_gain: bfloat16 [2, 2, 256], replicated, may hold values from 0.099609375 to 1.8984375
- narrow_bias: bfloat16 [2, 2, 256], replicated, may hold values from -3 to 3
- wide_gain: bfloat16 [2, 1024], replicated, may hold values from 0.099609375 to 1.8984375
- wide_bias: bfloat16 [2, 1024], replicated, may hold values from -3 to 3
Outputs:
- block_output: bfloat16 [672, 14, 14, 1024], P(('col', 'ta'))
- grad_frames: bfloat16 [672, 14, 14, 1024], P(('col', 'ta'))
- grad_w_reduce: float32 [2, 1024, 256], replicated
- grad_w_mid: float32 [2, 256, 256], replicated
- grad_depth_kernel: float32 [2, 27, 256], replicated
- grad_w_expand: float32 [2, 256, 1024], replicated
- grad_narrow_gain: float32 [2, 2, 256], replicated
- grad_narrow_bias: float32 [2, 2, 256], replicated
- grad_wide_gain: float32 [2, 1024], replicated
- grad_wide_bias: float32 [2, 1024], replicated
Inputs may be any that keep to these rules, and one draw needn't show every extreme that they name: `held`: devices 2i and 2i + 1 of ta hold 24 live frames together, in every clip group. `clip_stride`: in each group a quarter of the clips have stride 1 (8 frames), a quarter stride 2 (4 frames) and half stride 4 (2 frames), in any order.
All inputs are finite; a program needn't handle non-finite values.
Results may differ from a plain program's by a relative error of at most 0.017.
Values may be sent and summed in bfloat16 or wider, within the bound.
A program may use at most 320 MiB of HBM per device.

v0:
```python
import jax
import jax.numpy as jnp
from jax import lax
from jax.sharding import PartitionSpec as P

FR_DEV = 12


EPS = 1e-05


def extended(shard, sides, width):
    for axis, dim in sides:
        devices, length = (lax.axis_size(axis), shard.shape[dim])
        up = [(i, (i + 1) % devices) for i in range(devices - 1)]
        down = [(j, i) for i, j in up]
        last = lax.slice_in_dim(shard, length - width, length, axis=dim)
        first = lax.slice_in_dim(shard, 0, width, axis=dim)
        before = lax.ppermute(last, axis, up)
        after = lax.ppermute(first, axis, down)
        shard = jnp.concatenate([before, shard, after], axis=dim)
    return shard


def silu_slope(values):
    sigmoid_v = jax.nn.sigmoid(values)
    return sigmoid_v * (1.0 + values * (1.0 - sigmoid_v))


def normalize(values, alive_rows, summed_count, gain_vec, bias_vec):
    average = lax.psum(jnp.sum(values * alive_rows, axis=0), ("col", "ta")) / summed_count
    centred = values - average
    spread = lax.psum(jnp.sum(centred * centred * alive_rows, axis=0), ("col", "ta")) / summed_count
    inverse = lax.rsqrt(spread + EPS)
    normed = (values - average) * inverse
    return (normed, inverse, gain_vec * normed + bias_vec)


def normalize_back(grad_z, normed, inverse, gain_vec, alive_rows, summed_count):
    grad_bias, grad_gain = lax.psum(
        (jnp.sum(grad_z, axis=0), jnp.sum(grad_z * normed, axis=0)), ("col", "ta")
    )
    grad_input = (
        gain_vec * inverse * (grad_z - grad_bias / summed_count - normed * grad_gain / summed_count)
    )
    return (grad_input * alive_rows, grad_gain, grad_bias)


def padded_planes(source):
    return jnp.pad(source, ((0, 0), (1, 1), (1, 1), (0, 0)))


def spatial_apply(source, kernel, plane_id):
    padded = padded_planes(source)
    span_h, span_w = (source.shape[1], source.shape[2])
    result = jnp.zeros(source.shape, jnp.float32)
    for row_off in range(3):
        for col_off in range(3):
            result = (
                result
                + kernel[plane_id * 9 + row_off * 3 + col_off]
                * padded[:, row_off : row_off + span_h, col_off : col_off + span_w, :]
            )
    return result


def spatial_transpose(grid_grad, kernel, plane_id):
    padded = padded_planes(grid_grad)
    span_h, span_w = (grid_grad.shape[1], grid_grad.shape[2])
    result = jnp.zeros(grid_grad.shape, jnp.float32)
    for row_off in range(3):
        for col_off in range(3):
            result = (
                result
                + kernel[plane_id * 9 + row_off * 3 + col_off]
                * padded[
                    :, 2 - row_off : 2 - row_off + span_h, 2 - col_off : 2 - col_off + span_w, :
                ]
            )
    return result


def spatial_kernel_grad(grid_grad, source):
    padded = padded_planes(source)
    span_h, span_w = (source.shape[1], source.shape[2])
    rows_out = []
    for row_off in range(3):
        for col_off in range(3):
            rows_out.append(
                jnp.sum(
                    grid_grad
                    * padded[:, row_off : row_off + span_h, col_off : col_off + span_w, :],
                    axis=(0, 1, 2),
                )
            )
    return jnp.stack(rows_out)


def add_at(target, addend, position):
    current = lax.dynamic_slice_in_dim(target, position, 1, 0)
    return lax.dynamic_update_slice_in_dim(target, current + addend, position, 0)


def neighbour_masks(stride_row, first_frame, slots, count, frames_total):
    lengths = 8 // stride_row
    starts = jnp.cumsum(lengths) - lengths
    global_ids = first_frame + jnp.arange(slots)
    begins = jnp.sum((starts[None, :] == global_ids[:, None]).astype(jnp.int32), axis=1) > 0
    following = jnp.sum((starts[None, :] == global_ids[:, None] + 1).astype(jnp.int32), axis=1) > 0
    alive = jnp.arange(slots) < count
    prev_ok = alive & jnp.logical_not(begins)
    next_ok = alive & jnp.logical_not(following) & (global_ids + 1 < frames_total)
    return (alive, prev_ok, next_ok)


def body(
    frames,
    out_grad,
    held,
    clip_stride,
    w_reduce,
    w_mid,
    depth_kernel,
    w_expand,
    narrow_gain,
    narrow_bias,
    wide_gain,
    wide_bias,
):
    col_pos = lax.axis_index("col")
    ta_pos = lax.axis_index("ta")
    held_row = jnp.take(held, col_pos, axis=0)
    held_here = jnp.take(held_row, ta_pos)
    capacity, span_h, span_w, width = frames.shape
    pixels = span_h * span_w
    frames_total = held.shape[1] * FR_DEV
    summed_count = float(held.shape[0] * frames_total * pixels)
    arrival_alive = jnp.arange(capacity) < held_here
    grad_in = jnp.where(arrival_alive[:, None, None, None], out_grad, jnp.zeros((), out_grad.dtype))
    first_frame = jnp.sum(jnp.where(jnp.arange(held_row.shape[0]) < ta_pos, held_row, 0))
    slots = frames.shape[0]
    alive, prev_ok, next_ok = neighbour_masks(
        jnp.take(clip_stride, col_pos, axis=0), first_frame, slots, held_here, frames_total
    )
    alive_rows = jnp.repeat(alive.astype(jnp.float32), pixels)[:, None]
    alive_grid = alive.astype(jnp.float32)[:, None, None, None]
    prev_grid = prev_ok.astype(jnp.float32)[:, None, None, None]
    next_grid = next_ok.astype(jnp.float32)[:, None, None, None]
    bottleneck = w_mid.shape[1]
    zero_frame = jnp.zeros((1, span_h, span_w, bottleneck), jnp.bfloat16)
    act_low = frames.reshape(-1, width)
    act_full = act_low.astype(jnp.float32)
    saved = []
    for block_id in range(w_reduce.shape[0]):
        gains_narrow = narrow_gain[block_id].astype(jnp.float32)
        biases_narrow = narrow_bias[block_id].astype(jnp.float32)
        h_one = jnp.dot(act_low, w_reduce[block_id], preferred_element_type=jnp.float32)
        normed_one, inverse_one, z_one = normalize(
            h_one, alive_rows, summed_count, gains_narrow[0], biases_narrow[0]
        )
        u_one_low = jax.nn.silu(z_one).astype(jnp.bfloat16)
        h_two = jnp.dot(u_one_low, w_mid[block_id], preferred_element_type=jnp.float32).astype(
            jnp.bfloat16
        )
        grid = h_two.reshape(slots, span_h, span_w, bottleneck)
        rims = jnp.stack(
            [grid[0], lax.dynamic_index_in_dim(grid, held_here - 1, 0, keepdims=False)]
        )
        outer = extended(rims, (("ta", 0),), 1)
        earlier = jnp.concatenate([outer[0:1], grid[:-1]]).astype(jnp.float32) * prev_grid
        later_base = lax.dynamic_update_slice_in_dim(
            jnp.concatenate([grid[1:], zero_frame]), outer[3:4], held_here - 1, 0
        )
        later = later_base.astype(jnp.float32) * next_grid
        kernel = depth_kernel[block_id].astype(jnp.float32)
        sources = (earlier, grid.astype(jnp.float32), later)
        depth = (
            spatial_apply(sources[0], kernel, 0)
            + spatial_apply(sources[1], kernel, 1)
            + spatial_apply(sources[2], kernel, 2)
        )
        normed_two, inverse_two, z_two = normalize(
            depth.reshape(-1, bottleneck),
            alive_rows,
            summed_count,
            gains_narrow[1],
            biases_narrow[1],
        )
        u_two_low = jax.nn.silu(z_two).astype(jnp.bfloat16)
        h_three = jnp.dot(u_two_low, w_expand[block_id], preferred_element_type=jnp.float32)
        normed_three, inverse_three, z_three = normalize(
            h_three,
            alive_rows,
            summed_count,
            wide_gain[block_id].astype(jnp.float32),
            wide_bias[block_id].astype(jnp.float32),
        )
        pre_act = act_full + z_three
        saved.append(
            (
                act_low,
                normed_one,
                inverse_one,
                z_one,
                u_one_low,
                sources,
                normed_two,
                inverse_two,
                z_two,
                u_two_low,
                normed_three,
                inverse_three,
                pre_act,
            )
        )
        act_full = jax.nn.silu(pre_act)
        act_low = act_full.astype(jnp.bfloat16)
    grad_out = grad_in.reshape(-1, width).astype(jnp.float32)
    grads_reduce, grads_mid, grads_kernel, grads_expand = ([], [], [], [])
    grads_ngain, grads_nbias, grads_wgain, grads_wbias = ([], [], [], [])
    for block_id in reversed(range(w_reduce.shape[0])):
        (
            block_low,
            normed_one,
            inverse_one,
            z_one,
            u_one_low,
            sources,
            normed_two,
            inverse_two,
            z_two,
            u_two_low,
            normed_three,
            inverse_three,
            pre_act,
        ) = saved[block_id]
        gains_narrow = narrow_gain[block_id].astype(jnp.float32)
        kernel = depth_kernel[block_id].astype(jnp.float32)
        grad_pre = grad_out * silu_slope(pre_act)
        grad_h3, gain_three, bias_three = normalize_back(
            grad_pre,
            normed_three,
            inverse_three,
            wide_gain[block_id].astype(jnp.float32),
            alive_rows,
            summed_count,
        )
        grad_h3_low = grad_h3.astype(jnp.bfloat16)
        grads_expand.append(
            jnp.einsum("vc,vd->cd", u_two_low, grad_h3_low, preferred_element_type=jnp.float32)
        )
        grad_u2 = jnp.einsum(
            "vd,cd->vc", grad_h3_low, w_expand[block_id], preferred_element_type=jnp.float32
        )
        grad_depth, gain_two, bias_two = normalize_back(
            grad_u2 * silu_slope(z_two),
            normed_two,
            inverse_two,
            gains_narrow[1],
            alive_rows,
            summed_count,
        )
        grid_grad = grad_depth.reshape(slots, span_h, span_w, bottleneck)
        grads_kernel.append(
            jnp.concatenate(
                [
                    spatial_kernel_grad(grid_grad, sources[0]),
                    spatial_kernel_grad(grid_grad, sources[1]),
                    spatial_kernel_grad(grid_grad, sources[2]),
                ]
            )
        )
        toward_prev = spatial_transpose(grid_grad, kernel, 0) * prev_grid
        toward_self = spatial_transpose(grid_grad, kernel, 1)
        toward_next = spatial_transpose(grid_grad, kernel, 2) * next_grid
        rims_back = jnp.stack(
            [
                toward_prev[0],
                lax.dynamic_index_in_dim(toward_next, held_here - 1, 0, keepdims=False),
            ]
        )
        outer_back = extended(rims_back.astype(jnp.bfloat16), (("ta", 0),), 1).astype(
            rims_back.dtype
        )
        zero_grad = jnp.zeros((1, span_h, span_w, bottleneck), jnp.float32)
        from_later = add_at(
            jnp.concatenate([toward_prev[1:], zero_grad]), outer_back[3:4], held_here - 1
        )
        from_earlier = add_at(jnp.concatenate([zero_grad, toward_next[:-1]]), outer_back[0:1], 0)
        grad_h2 = (
            ((toward_self + from_later + from_earlier) * alive_grid)
            .reshape(-1, bottleneck)
            .astype(jnp.bfloat16)
        )
        grads_mid.append(
            jnp.einsum("vc,vd->cd", u_one_low, grad_h2, preferred_element_type=jnp.float32)
        )
        grad_u1 = jnp.einsum(
            "vd,cd->vc", grad_h2, w_mid[block_id], preferred_element_type=jnp.float32
        )
        grad_h1, gain_one, bias_one = normalize_back(
            grad_u1 * silu_slope(z_one),
            normed_one,
            inverse_one,
            gains_narrow[0],
            alive_rows,
            summed_count,
        )
        grad_h1_low = grad_h1.astype(jnp.bfloat16)
        grads_reduce.append(
            jnp.einsum("vc,vd->cd", block_low, grad_h1_low, preferred_element_type=jnp.float32)
        )
        grad_out = (
            jnp.einsum(
                "vb,db->vd", grad_h1_low, w_reduce[block_id], preferred_element_type=jnp.float32
            )
            + grad_pre
        )
        grads_ngain.append(jnp.stack([gain_one, gain_two]))
        grads_nbias.append(jnp.stack([bias_one, bias_two]))
        grads_wgain.append(gain_three)
        grads_wbias.append(bias_three)
    out_low = act_full.reshape(slots, span_h, span_w, width).astype(jnp.bfloat16)
    grad_low = grad_out.reshape(slots, span_h, span_w, width).astype(jnp.bfloat16)
    block_output = jnp.where(
        arrival_alive[:, None, None, None], out_low, jnp.zeros((), jnp.bfloat16)
    )
    grad_frames = jnp.where(
        arrival_alive[:, None, None, None], grad_low, jnp.zeros((), jnp.bfloat16)
    )
    summed_reduce, summed_mid, summed_kernel, summed_expand = lax.psum(
        (
            jnp.stack(grads_reduce[::-1]),
            jnp.stack(grads_mid[::-1]),
            jnp.stack(grads_kernel[::-1]),
            jnp.stack(grads_expand[::-1]),
        ),
        ("col", "ta"),
    )
    return (
        block_output,
        grad_frames,
        summed_reduce,
        summed_mid,
        summed_kernel,
        summed_expand,
        jnp.stack(grads_ngain[::-1]),
        jnp.stack(grads_nbias[::-1]),
        jnp.stack(grads_wgain[::-1]),
        jnp.stack(grads_wbias[::-1]),
    )


def solution(mesh):
    placed = (
        P(("col", "ta"), None, None, None),
        P(("col", "ta"), None, None, None),
        P(),
        P(),
        P(),
        P(),
        P(),
        P(),
        P(),
        P(),
        P(),
        P(),
    )
    return jax.shard_map(
        body,
        mesh=mesh,
        in_specs=placed,
        out_specs=(
            P(("col", "ta"), None, None, None),
            P(("col", "ta"), None, None, None),
            P(),
            P(),
            P(),
            P(),
            P(),
            P(),
            P(),
            P(),
        ),
        check_vma=False,
    )
```

profile of v0, /device:TPU:0, one launch (start us, length us, event | category | flops | bytes accessed | tf_op | source)
XLA Modules:
  0.0 1641.1 jit_solution(1639509669055725143)
XLA Ops:
  10.0 12.9 reshape.475
  30.7 42.0 %psum.196 = f32[256]{0:T(256)S(1)} all-reduce(f32[256]{0:T(256)S(1)} %get-tuple-element.276), channel_id=1, replica_groups=mesh['col'=4,'ta'=8] {'col','ta'}, use_global_device_ids=true, to_apply=%region_1.2 | all-reduce | flops 256 | bytes 2048 | tf_op jit(solution)/shard_map/psum | solution.py:31
  76.1 40.2 %psum.197 = f32[256]{0:T(256)S(1)} all-reduce(f32[256]{0:T(256)S(1)} %multiply_reduce_fusion.70), channel_id=1, replica_groups=mesh['col'=4,'ta'=8] {'col','ta'}, use_global_device_ids=true, to_apply=%region_3.4 | all-reduce | flops 256 | bytes 2048 | tf_op jit(solution)/shard_map/psum | solution.py:33
  157.6 18.5 %reshape.564 = f32[4116,1024]{1,0:T(8,128)} reshape(f32[21,14,14,1024]{3,2,1,0:T(8,128)} %select_convert_fusion) | data formatting | bytes 33718272 | tf_op jit(solution)/shard_map/convert_element_type | solution.py:218
  185.2 60.1 %multiply_reduce_fusion.59 = (f32[256]{0:T(256)S(1)}, f32[21,14,14,256]{3,2,1,0:T(8,128)}) fusion(f32[21]{0:T(128)S(1)} %fusion.67, f32[256]{0:T(256)S(1)} %bitcast.279, f32[256]{0:T(256)S(1)} %bitcast.281, f32[256]{0:T(256)S(1)} %bitcast.283, f32[256]{0:T(256)S(1)} %bitcast.285, f32[21,14,14,256]{3,2,1,0:T(8,128)} %convert_multiply_fusion.1, ...), kind=kLoop, calls=%fused_computation.159 | loop fusion | flops 57953024 | bytes 16887892 | tf_op jit(solution)/shard_map/reduce_sum | solution.py:31
  245.4 43.0 %psum.198 = f32[256]{0:T(256)S(1)} all-reduce(f32[256]{0:T(256)S(1)} %get-tuple-element.178), channel_id=1, replica_groups=mesh['col'=4,'ta'=8] {'col','ta'}, use_global_device_ids=true, to_apply=%region_9.10 | all-reduce | flops 256 | bytes 2048 | tf_op jit(solution)/shard_map/psum | solution.py:31
  291.7 40.4 %psum.199 = f32[256]{0:T(256)S(1)} all-reduce(f32[256]{0:T(256)S(1)} %multiply_reduce_fusion.58), channel_id=1, replica_groups=mesh['col'=4,'ta'=8] {'col','ta'}, use_global_device_ids=true, to_apply=%region_11.12 | all-reduce | flops 256 | bytes 2048 | tf_op jit(solution)/shard_map/psum | solution.py:33
  348.3 40.1 %psum.200 = f32[1024]{0:T(1024)S(1)} all-reduce(f32[1024]{0:T(1024)S(1)} %get-tuple-element.278), channel_id=1, replica_groups=mesh['col'=4,'ta'=8] {'col','ta'}, use_global_device_ids=true, to_apply=%region_13.14 | all-reduce | flops 1024 | bytes 8192 | tf_op jit(solution)/shard_map/psum | solution.py:31
  395.6 40.0 %psum.201 = f32[1024]{0:T(1024)S(1)} all-reduce(f32[1024]{0:T(1024)S(1)} %multiply_reduce_fusion.4), channel_id=1, replica_groups=mesh['col'=4,'ta'=8] {'col','ta'}, use_global_device_ids=true, to_apply=%region_15.16 | all-reduce | flops 1024 | bytes 8192 | tf_op jit(solution)/shard_map/psum | solution.py:33
  454.2 40.2 %psum.202 = f32[256]{0:T(256)S(1)} all-reduce(f32[256]{0:T(256)S(1)} %get-tuple-element.280), channel_id=1, replica_groups=mesh['col'=4,'ta'=8] {'col','ta'}, use_global_device_ids=true, to_apply=%region_17.18 | all-reduce | flops 256 | bytes 2048 | tf_op jit(solution)/shard_map/psum | solution.py:31
  497.8 40.0 %psum.203 = f32[256]{0:T(256)S(1)} all-reduce(f32[256]{0:T(256)S(1)} %multiply_reduce_fusion.68), channel_id=1, replica_groups=mesh['col'=4,'ta'=8] {'col','ta'}, use_global_device_ids=true, to_apply=%region_19.20 | all-reduce | flops 256 | bytes 2048 | tf_op jit(solution)/shard_map/psum | solution.py:33
  587.2 59.2 %multiply_reduce_fusion.57 = (f32[256]{0:T(256)S(1)}, f32[21,14,14,256]{3,2,1,0:T(8,128)}) fusion(f32[21]{0:T(128)S(1)} %fusion.67, f32[256]{0:T(256)S(1)} %bitcast.349, f32[256]{0:T(256)S(1)} %bitcast.351, f32[256]{0:T(256)S(1)} %bitcast.353, f32[256]{0:T(256)S(1)} %bitcast.355, f32[21,14,14,256]{3,2,1,0:T(8,128)} %convert_multiply_fusion, ...), kind=kLoop, calls=%fused_computation.154 | loop fusion | flops 57953024 | bytes 16887892 | tf_op jit(solution)/shard_map/reduce_sum | solution.py:31
  646.4 43.3 %psum.204 = f32[256]{0:T(256)S(1)} all-reduce(f32[256]{0:T(256)S(1)} %get-tuple-element.176), channel_id=1, replica_groups=mesh['col'=4,'ta'=8] {'col','ta'}, use_global_device_ids=true, to_apply=%region_21.22 | all-reduce | flops 256 | bytes 2048 | tf_op jit(solution)/shard_map/psum | solution.py:31
  698.4 40.0 %psum.205 = f32[256]{0:T(256)S(1)} all-reduce(f32[256]{0:T(256)S(1)} %multiply_reduce_fusion.56), channel_id=1, replica_groups=mesh['col'=4,'ta'=8] {'col','ta'}, use_global_device_ids=true, to_apply=%region_23.24 | all-reduce | flops 256 | bytes 2048 | tf_op jit(solution)/shard_map/psum | solution.py:33
  754.0 40.1 %psum.206 = f32[1024]{0:T(1024)S(1)} all-reduce(f32[1024]{0:T(1024)S(1)} %get-tuple-element.282), channel_id=1, replica_groups=mesh['col'=4,'ta'=8] {'col','ta'}, use_global_device_ids=true, to_apply=%region_25.26 | all-reduce | flops 1024 | bytes 8192 | tf_op jit(solution)/shard_map/psum | solution.py:31
  801.3 40.4 %psum.207 = f32[1024]{0:T(1024)S(1)} all-reduce(f32[1024]{0:T(1024)S(1)} %multiply_reduce_fusion.2), channel_id=1, replica_groups=mesh['col'=4,'ta'=8] {'col','ta'}, use_global_device_ids=true, to_apply=%region_27.28 | all-reduce | flops 1024 | bytes 8192 | tf_op jit(solution)/shard_map/psum | solution.py:33
  841.8 25.8 %fusion.69 = (f32[1024]{0:T(1024)S(1)}, f32[1024]{0:T(1024)S(1)}, f32[4116,1024]{1,0:T(8,128)}, bf16[4116,1024]{1,0:T(8,128)(2,1)}) fusion(f32[1024]{0:T(1024)S(1)} %get-tuple-element.249, f32[4116,1024]{1,0:T(8,128)} %get-tuple-element.283, f32[1024]{0:T(1024)S(1)} %broadcast_multiply_fusion.4, f32[4116,1024]{1,0:T(8,128)} %reshape.564, ...), kind=kLoop, calls=%fused_computation.336 | loop fusion | flops 75864064 | bytes 75890688 | tf_op jit(solution)/shard_map/reduce_sum | solution.py:41
  867.6 40.1 %all-reduce.17 = (f32[1024]{0:T(1024)S(1)}, f32[1024]{0:T(1024)S(1)}) all-reduce(f32[1024]{0:T(1024)S(1)} %get-tuple-element.76, f32[1024]{0:T(1024)S(1)} %get-tuple-element.75), channel_id=1, replica_groups=mesh['col'=4,'ta'=8] {'col','ta'}, use_global_device_ids=true, to_apply=%region_31.32 | all-reduce | flops 2048 | bytes 16384 | tf_op jit(solution)/shard_map/psum | solution.py:40
  929.1 40.2 %all-reduce.16 = (f32[256]{0:T(256)S(1)}, f32[256]{0:T(256)S(1)}) all-reduce(f32[256]{0:T(256)S(1)} %get-tuple-element.154, f32[256]{0:T(256)S(1)} %get-tuple-element.153), channel_id=1, replica_groups=mesh['col'=4,'ta'=8] {'col','ta'}, use_global_device_ids=true, to_apply=%region_35.36 | all-reduce | flops 512 | bytes 4096 | tf_op jit(solution)/shard_map/psum | solution.py:40
  989.9 22.5 %add_multiply_fusion.3 = f32[21,14,14,256]{3,2,1,0:T(8,128)} fusion(f32[21,14,14,256]{3,2,1,0:T(8,128)} %reshape.480, f32[256]{0:T(256)S(1)} %bitcast.336, f32[256]{0:T(256)S(1)} %bitcast.338, f32[256]{0:T(256)S(1)} %bitcast.340, f32[256]{0:T(256)S(1)} %bitcast.342, f32[256]{0:T(256)S(1)} %bitcast.344, f32[256]{0:T(256)S(1)} %bitcast.346, ...), kind=kLoop, calls=%fused_computation.151 | loop fusion | flops 18966528 | bytes 8438868 | tf_op jit(solution)/shard_map/mul | solution.py:273
  1019.7 20.2 %multiply_reduce_fusion.6 = (f32[256]{0:T(256)S(1)}, f32[256]{0:T(256)S(1)}, f32[256]{0:T(256)S(1)}, f32[256]{0:T(256)S(1)}, f32[256]{0:T(256)S(1)}, /*index=5*/...) fusion(f32[21,14,14,256]{3,2,1,0:T(8,128)S(1)} %copy-done.2, ...), kind=kLoop, calls=%fused_computation.98 | loop fusion | flops 37928704 | bytes 14769236 | tf_op jit(solution)/shard_map/reduce_sum | solution.py:90
  1089.7 23.9 %fusion.2 = bf16[21,14,14,256]{3,2,1,0:T(8,128)(2,1)S(1)} fusion(f32[20,14,14,256]{3,2,1,0:T(8,128)} %slice.987, f32[1,14,14,256]{3,2,1,0:T(8,128)S(1)} %fusion.56, f32[21,14,14,256]{3,2,1,0:T(8,128)} %fusion.46, f32[21,14,14,256]{3,2,1,0:T(8,128)} %reshape.480, f32[256]{0:T(256)S(1)} %bitcast.316, f32[256]{0:T(256)S(1)} %bitcast.318, f32[256]{0:T(256)S(1)} %bitcast.320, ...), kind=kLoop, calls=%fused_computation.94 | loop fusion | flops 23181312 | bytes 14761044 | tf_op jit(solution)/shard_map/convert_element_type | solution.py:293
  1121.7 40.4 %all-reduce.15 = (f32[256]{0:T(256)S(1)}, f32[256]{0:T(256)S(1)}) all-reduce(f32[256]{0:T(256)S(1)} %get-tuple-element.152, f32[256]{0:T(256)S(1)} %get-tuple-element.151), channel_id=1, replica_groups=mesh['col'=4,'ta'=8] {'col','ta'}, use_global_device_ids=true, to_apply=%region_39.40 | all-reduce | flops 512 | bytes 4096 | tf_op jit(solution)/shard_map/psum | solution.py:40
  1167.3 22.6 %fusion.68 = (f32[1024]{0:T(1024)S(1)}, f32[1024]{0:T(1024)S(1)}, f32[4116,1024]{1,0:T(8,128)}) fusion(f32[1024]{0:T(1024)S(1)} %copy-done.48, f32[4116,1024]{1,0:T(8,128)} %get-tuple-element.279, f32[1024]{0:T(1024)S(1)} %copy-done.44, f32[1024]{0:T(1024)S(1)} %bitcast.255, f32[1024]{0:T(1024)S(1)} %bitcast.251, bf16[4116,1024]{1,0:T(8,128)(2,1)} %reshape.475, ...), kind=kOutput, calls=%fused_computation.335 | convolution fusion | flops 2233833472 | bytes 61665280 | tf_op jit(solution)/shard_map/vb,db->vd/dot_general | solution.py:314
  1189.9 40.0 %all-reduce.14 = (f32[1024]{0:T(1024)S(1)}, f32[1024]{0:T(1024)S(1)}) all-reduce(f32[1024]{0:T(1024)S(1)} %get-tuple-element.74, f32[1024]{0:T(1024)S(1)} %get-tuple-element.73), channel_id=1, replica_groups=mesh['col'=4,'ta'=8] {'col','ta'}, use_global_device_ids=true, to_apply=%region_43.44 | all-reduce | flops 2048 | bytes 16384 | tf_op jit(solution)/shard_map/psum | solution.py:40
  1251.4 40.2 %all-reduce.13 = (f32[256]{0:T(256)S(1)}, f32[256]{0:T(256)S(1)}) all-reduce(f32[256]{0:T(256)S(1)} %get-tuple-element.150, f32[256]{0:T(256)S(1)} %get-tuple-element.149), channel_id=1, replica_groups=mesh['col'=4,'ta'=8] {'col','ta'}, use_global_device_ids=true, to_apply=%region_47.48 | all-reduce | flops 512 | bytes 4096 | tf_op jit(solution)/shard_map/psum | solution.py:40
  1304.8 30.4 %multiply_reduce_fusion.31 = (f32[256]{0:T(256)S(1)}, f32[256]{0:T(256)S(1)}, f32[256]{0:T(256)S(1)}, f32[256]{0:T(256)S(1)}, f32[256]{0:T(256)S(1)}, /*index=5*...) fusion(f32[21,14,14,256]{3,2,1,0:T(8,128)} %reshape.482, ...), kind=kLoop, calls=%fused_computation.123 | loop fusion | flops 37928704 | bytes 14769236 | tf_op jit(solution)/shard_map/reduce_sum | solution.py:90
  1394.3 24.1 %fusion.4 = bf16[21,14,14,256]{3,2,1,0:T(8,128)(2,1)} fusion(f32[20,14,14,256]{3,2,1,0:T(8,128)} %slice.990, f32[1,14,14,256]{3,2,1,0:T(8,128)} %fusion.55, f32[21,14,14,256]{3,2,1,0:T(8,128)S(1)} %fusion.45, f32[21,14,14,256]{3,2,1,0:T(8,128)} %reshape.482, f32[21]{0:T(128)S(1)} %fusion.67, f32[256]{0:T(256)S(1)} %bitcast.262, f32[256]{0:T(256)} %bitcast.264, ...), kind=kLoop, calls=%fused_computation.97 | loop fusion | flops 23181312 | bytes 14761044 | tf_op jit(solution)/shard_map/convert_element_type | solution.py:293
  1428.2 40.7 %all-reduce.12 = (f32[256]{0:T(256)S(1)}, f32[256]{0:T(256)S(1)}, f32[2,27,256]{2,1,0:T(8,128)S(1)}) all-reduce(f32[256]{0:T(256)S(1)} %get-tuple-element.148, f32[256]{0:T(256)S(1)} %get-tuple-element.147, f32[2,27,256]{2,1,0:T(8,128)S(1)} %copy-done.39), channel_id=1, replica_groups=mesh['col'=4,'ta'=8] {'col','ta'}, use_global_device_ids=true, to_apply=%region_51.52 | all-reduce | flops 14336 | bytes 114688 | tf_op jit(solution)/shard_map/psum | solution.py:40
  1493.1 12.8 convert_element_type.251
  1507.8 14.3 broadcast_select_fusion
  1522.1 105.4 %all-reduce.21.cloned.1.call-done = (f32[2,1024,256]{1,2,0:T(8,128)}, f32[2,256,256]{2,1,0:T(8,128)}, f32[2,256,1024]{2,1,0:T(8,128)}) async-done(((f32[2,1024,256]{1,2,0:T(8,128)}, f32[2,256,256]{2,1,0:T(8,128)}, f32[2,256,1024]{2,1,0:T(8,128)}), (f32[2,1024,256]{1,2,0:T(8,128)}, f32[2,256,256]{2,1,0:T(8,128)}, f32[2,256,1024]{2,1,0:T(8,128)})) %all-reduce.21.cloned.1.call-update) | async-done | bytes 4718608 | tf_op jit(solution)/shard_map/psum | solution.py:331
  (474 shorter events, 440.0 us)
Async XLA Ops:
  7.2 1620.4 %all-reduce.21.cloned.1.call-start = ((), (), s32[]{:S(2)}) async-start(), calls=%async_computation | async-start | bytes 9437184 | tf_op jit(solution)/shard_map/psum | solution.py:331
  22.9 93.4 %copy-start.133 = (bf16[2,2,256]{2,1,0:T(2,128)(2,1)S(1)}, bf16[2,2,256]{2,1,0:T(2,128)(2,1)}, u32[]{:S(2)}) copy-start(bf16[2,2,256]{2,1,0:T(2,128)(2,1)} %param.20) | copy-start | bytes 6148
  22.9 93.4 %copy-start.134 = (bf16[2,2,256]{2,1,0:T(2,128)(2,1)S(1)}, bf16[2,2,256]{2,1,0:T(2,128)(2,1)}, u32[]{:S(2)}) copy-start(bf16[2,2,256]{2,1,0:T(2,128)(2,1)} %param.21) | copy-start | bytes 6148
  116.9 215.8 %copy-start.118 = (f32[1,1,256]{2,1,0:T(1,128)}, f32[1,1,256]{2,1,0:T(1,128)S(1)}, u32[]{:S(2)}) copy-start(f32[1,1,256]{2,1,0:T(1,128)S(1)} %get-tuple-element.302) | copy-start | bytes 3076
  126.7 55.2 %collective-permute-start = (bf16[1,14,14,256]{3,2,1,0:T(8,128)(2,1)S(1)}, bf16[1,14,14,256]{3,2,1,0:T(8,128)(2,1)S(1)}, u32[]{:S(2)}, u32[]{:S(2)}) collective-permute-start(bf16[1,14,14,256]{3,2,1,0:T(8,128)(2,1)S(1)} %constant_dynamic-slice_fusion.4), channel_id=1, source_target_pairs={{0,1},{1,2},{2,3},{3,4},{4,5},{5,6},{6,7},{8,9},{9,10},{10,11},{11... | collective-permute-start | bytes 301064 | tf_op jit(solution)/shard_map/ppermute | solution.py:19
  128.1 50.8 %collective-permute-start.1 = (bf16[1,14,14,256]{3,2,1,0:T(8,128)(2,1)S(1)}, bf16[1,14,14,256]{3,2,1,0:T(8,128)(2,1)S(1)}, u32[]{:S(2)}, u32[]{:S(2)}) collective-permute-start(bf16[1,14,14,256]{3,2,1,0:T(8,128)(2,1)S(1)} %slice.781), channel_id=1, source_target_pairs={{1,0},{2,1},{3,2},{4,3},{5,4},{6,5},{7,6},{9,8},{10,9},{11,10},{12... | collective-permute-start | bytes 301064 | tf_op jit(solution)/shard_map/ppermute | solution.py:20
  133.5 51.5 %copy-start.64 = (f32[1,1,256]{2,0,1:T(1,128)}, f32[1,1,256]{2,0,1:T(1,128)S(1)}, u32[]{:S(2)}) copy-start(f32[1,1,256]{2,0,1:T(1,128)S(1)} %get-tuple-element.229) | copy-start | bytes 3076
  133.5 51.5 %copy-start.66 = (f32[1,1,256]{2,0,1:T(1,128)}, f32[1,1,256]{2,0,1:T(1,128)S(1)}, u32[]{:S(2)}) copy-start(f32[1,1,256]{2,0,1:T(1,128)S(1)} %get-tuple-element.230) | copy-start | bytes 3076
  133.5 51.5 %copy-start.67 = (f32[1,1,256]{2,0,1:T(1,128)}, f32[1,1,256]{2,0,1:T(1,128)S(1)}, u32[]{:S(2)}) copy-start(f32[1,1,256]{2,0,1:T(1,128)S(1)} %get-tuple-element.231) | copy-start | bytes 3076
  133.5 51.5 %copy-start.68 = (f32[1,1,256]{2,0,1:T(1,128)}, f32[1,1,256]{2,0,1:T(1,128)S(1)}, u32[]{:S(2)}) copy-start(f32[1,1,256]{2,0,1:T(1,128)S(1)} %get-tuple-element.232) | copy-start | bytes 3076
  133.5 51.5 %copy-start.69 = (f32[1,1,256]{2,0,1:T(1,128)}, f32[1,1,256]{2,0,1:T(1,128)S(1)}, u32[]{:S(2)}) copy-start(f32[1,1,256]{2,0,1:T(1,128)S(1)} %get-tuple-element.233) | copy-start | bytes 3076
  133.5 51.5 %copy-start.70 = (f32[1,1,256]{2,0,1:T(1,128)}, f32[1,1,256]{2,0,1:T(1,128)S(1)}, u32[]{:S(2)}) copy-start(f32[1,1,256]{2,0,1:T(1,128)S(1)} %get-tuple-element.234) | copy-start | bytes 3076
  133.5 51.5 %copy-start.71 = (f32[1,1,256]{2,0,1:T(1,128)}, f32[1,1,256]{2,0,1:T(1,128)S(1)}, u32[]{:S(2)}) copy-start(f32[1,1,256]{2,0,1:T(1,128)S(1)} %get-tuple-element.235) | copy-start | bytes 3076
  133.5 51.5 %copy-start.72 = (f32[1,1,256]{2,0,1:T(1,128)}, f32[1,1,256]{2,0,1:T(1,128)S(1)}, u32[]{:S(2)}) copy-start(f32[1,1,256]{2,0,1:T(1,128)S(1)} %get-tuple-element.236) | copy-start | bytes 3076
  133.5 51.5 %copy-start.73 = (f32[1,1,256]{2,0,1:T(1,128)}, f32[1,1,256]{2,0,1:T(1,128)S(1)}, u32[]{:S(2)}) copy-start(f32[1,1,256]{2,0,1:T(1,128)S(1)} %get-tuple-element.237) | copy-start | bytes 3076
  133.6 51.5 %copy-start.74 = (f32[1,1,256]{2,0,1:T(1,128)}, f32[1,1,256]{2,0,1:T(1,128)S(1)}, u32[]{:S(2)}) copy-start(f32[1,1,256]{2,0,1:T(1,128)S(1)} %get-tuple-element.220) | copy-start | bytes 3076
  133.6 51.5 %copy-start.76 = (f32[1,1,256]{2,0,1:T(1,128)}, f32[1,1,256]{2,0,1:T(1,128)S(1)}, u32[]{:S(2)}) copy-start(f32[1,1,256]{2,0,1:T(1,128)S(1)} %get-tuple-element.221) | copy-start | bytes 3076
  133.6 51.5 %copy-start.78 = (f32[1,1,256]{2,0,1:T(1,128)}, f32[1,1,256]{2,0,1:T(1,128)S(1)}, u32[]{:S(2)}) copy-start(f32[1,1,256]{2,0,1:T(1,128)S(1)} %get-tuple-element.222) | copy-start | bytes 3076
  133.6 51.5 %copy-start.80 = (f32[1,1,256]{2,0,1:T(1,128)}, f32[1,1,256]{2,0,1:T(1,128)S(1)}, u32[]{:S(2)}) copy-start(f32[1,1,256]{2,0,1:T(1,128)S(1)} %get-tuple-element.223) | copy-start | bytes 3076
  133.6 51.5 %copy-start.82 = (f32[1,1,256]{2,0,1:T(1,128)}, f32[1,1,256]{2,0,1:T(1,128)S(1)}, u32[]{:S(2)}) copy-start(f32[1,1,256]{2,0,1:T(1,128)S(1)} %get-tuple-element.224) | copy-start | bytes 3076
  133.6 51.5 %copy-start.84 = (f32[1,1,256]{2,0,1:T(1,128)}, f32[1,1,256]{2,0,1:T(1,128)S(1)}, u32[]{:S(2)}) copy-start(f32[1,1,256]{2,0,1:T(1,128)S(1)} %get-tuple-element.225) | copy-start | bytes 3076
  133.6 51.5 %copy-start.86 = (f32[1,1,256]{2,0,1:T(1,128)}, f32[1,1,256]{2,0,1:T(1,128)S(1)}, u32[]{:S(2)}) copy-start(f32[1,1,256]{2,0,1:T(1,128)S(1)} %get-tuple-element.226) | copy-start | bytes 3076
  133.6 51.5 %copy-start.88 = (f32[1,1,256]{2,0,1:T(1,128)}, f32[1,1,256]{2,0,1:T(1,128)S(1)}, u32[]{:S(2)}) copy-start(f32[1,1,256]{2,0,1:T(1,128)S(1)} %get-tuple-element.227) | copy-start | bytes 3076
  134.9 301.4 %copy-start.45 = (f32[1,1024]{1,0:T(1,128)}, f32[1,1024]{1,0:T(1,128)S(1)}, u32[]{:S(2)}) copy-start(f32[1,1024]{1,0:T(1,128)S(1)} %get-tuple-element.251) | copy-start | bytes 12292
  134.9 301.3 %copy-start.55 = (f32[1,1024]{1,0:T(1,128)}, f32[1,1024]{1,0:T(1,128)S(1)}, u32[]{:S(2)}) copy-start(f32[1,1024]{1,0:T(1,128)S(1)} %get-tuple-element.253) | copy-start | bytes 12292
  564.3 19.6 %collective-permute-start.2 = (bf16[1,14,14,256]{3,2,1,0:T(8,128)(2,1)S(1)}, bf16[1,14,14,256]{3,2,1,0:T(8,128)(2,1)S(1)}, u32[]{:S(2)}, u32[]{:S(2)}) collective-permute-start(bf16[1,14,14,256]{3,2,1,0:T(8,128)(2,1)S(1)} %constant_dynamic-slice_fusion.3), channel_id=1, source_target_pairs={{0,1},{1,2},{2,3},{3,4},{4,5},{5,6},{6,7},{8,9},{9,10},{10,11},{11... | collective-permute-start | bytes 301064 | tf_op jit(solution)/shard_map/ppermute | solution.py:19
  565.6 15.3 collective-permute-start.3
  1049.4 38.6 %collective-permute-start.5 = (bf16[1,14,14,256]{3,2,1,0:T(8,128)(2,1)S(1)}, bf16[1,14,14,256]{3,2,1,0:T(8,128)(2,1)S(1)}, u32[]{:S(2)}, u32[]{:S(2)}) collective-permute-start(bf16[1,14,14,256]{3,2,1,0:T(8,128)(2,1)S(1)} %slice.1406), channel_id=1, source_target_pairs={{1,0},{2,1},{3,2},{4,3},{5,4},{6,5},{7,6},{9,8},{10,9},{11,10},{12... | collective-permute-start | bytes 301064 | tf_op jit(solution)/shard_map/ppermute | solution.py:20
  1051.6 36.3 %collective-permute-start.4 = (bf16[1,14,14,256]{3,2,1,0:T(8,128)(2,1)S(1)}, bf16[1,14,14,256]{3,2,1,0:T(8,128)(2,1)S(1)}, u32[]{:S(2)}, u32[]{:S(2)}) collective-permute-start(bf16[1,14,14,256]{3,2,1,0:T(8,128)(2,1)S(1)} %dynamic-slice_convert_fusion.1), channel_id=1, source_target_pairs={{0,1},{1,2},{2,3},{3,4},{4,5},{5,6},{6,7},{8,9},{9,10},{10,11},{11... | collective-permute-start | bytes 301064 | tf_op jit(solution)/shard_map/ppermute | solution.py:19
  1167.3 62.6 %copy-start.61 = (f32[1024]{0:T(1024)S(1)}, f32[1024]{0:T(1024)}, u32[]{:S(2)}) copy-start(f32[1024]{0:T(1024)} %get-tuple-element.246) | copy-start | bytes 12292
  1379.8 11.9 collective-permute-start.7
  1381.2 10.5 collective-permute-start.6
  (127 other events, 2094.0 us)
Sparse Core Ops, SparseCore 0:
  1481.8 145.7 all-reduce.20
where the time goes:
time: 1650 us; the launch traced here: 1640 us
  blocking collectives  731 us (44%)
  other arithmetic  475 us (29%)
  local copies, waits for them, and re-layouts  171 us (10%)
  matrix products  126 us (8%)
  waiting for transfers between devices  105 us (6%)
  between operations  17.1 us (1%)
    psum x6, blocking collectives, normalize(): lax.psum(jnp.sum(values * alive_rows, axis=0), ('col', 'ta')) / summed_count  249 us
    psum x6, blocking collectives, normalize_back(): lax.psum((jnp.sum(grad_z, axis=0), jnp.sum(grad_z * normed, axis=0)), ('c...  242 us
    psum x6, blocking collectives, normalize(): lax.psum(jnp.sum(centred * centred * alive_rows, axis=0), ('col', 'ta'))  241 us
    reduce_sum x2, other arithmetic, normalize(): jnp.sum(values * alive_rows, axis=0)  119 us
    psum x1, waiting for transfers between devices, body(): lax.psum((jnp.stack(grads_reduce[::-1]), jnp.stack(grads_mid[::-1]), jnp....  105 us
    reduce_sum x6, other arithmetic, spatial_kernel_grad(): jnp.sum(grid_grad * padded[:, row_off:row_off + span_h, col_off:col_off +...  78.9 us
    convert_element_type x2, other arithmetic, body(): grad_h2 = ((toward_self + from_later + from_earlier) * alive_grid).reshap...  48 us
    dot_general x2, matrix products, body(): jnp.einsum('vb,db->vd', grad_h1_low, w_reduce[block_id], preferred_elemen...  34.1 us
  transfers between devices with their start and end apart: 9, of which 1 were waited for; matrix products, arithmetic and copies ran while one was open for 9% of the time, Pallas kernels for 0%

commit v1 on v0

v1 whole, which is shorter than its diff:
```python
import functools

import jax
import jax.numpy as jnp
from jax import lax
from jax.experimental import pallas as pl
from jax.experimental.pallas import tpu as pltpu
from jax.sharding import PartitionSpec as P

FR = 12
EPS = 1e-05
MESH = pl.DeviceIdType.MESH
F32 = jnp.float32
BF16 = jnp.bfloat16
ANY = pl.BlockSpec(memory_space=pl.ANY)
VM = pl.BlockSpec(memory_space=pltpu.VMEM)
SM = pl.BlockSpec(memory_space=pltpu.SMEM)


def loop(low, high, step):
    lax.fori_loop(low, high, step, 0)


def dot_nn(left, right):
    return lax.dot_general(left, right, (((1,), (0,)), ((), ())), preferred_element_type=F32)


def dot_nt(left, right):
    return lax.dot_general(left, right, (((1,), (1,)), ((), ())), preferred_element_type=F32)


def dot_tn(left, right):
    return lax.dot_general(left, right, (((0,), (0,)), ((), ())), preferred_element_type=F32)


def silu(values):
    half = 0.5 * values
    return half * jnp.tanh(half) + half


def silu_and_slope(values):
    half = 0.5 * values
    tan = jnp.tanh(half)
    act = half * tan + half
    sig = 0.5 * tan + 0.5
    return act, act + sig * (1.0 - act)


def main_kernel(
    dims,
    held,
    okmask,
    frames,
    gout,
    w1,
    w2,
    w3,
    taps,
    ngain,
    nbias,
    wgain,
    wbias,
    a2w,
    a2r,
    gw,
    gr,
    o_w1t,
    o_w2,
    o_w3,
    o_k,
    o_ng,
    o_nb,
    o_wg,
    o_wb,
    pool,
    a0,
    a1,
    pbuf,
    tile,
    ost,
    u2b,
    hbuf,
    x1b,
    x2b,
    cbuf,
    dbuf,
    dhb,
    wacc,
    w2acc,
    kacc,
    nbuf,
    tbuf,
    gbuf,
    sacc,
    prm,
    in_sem,
    rem_sem,
    halo_sem,
    out_sem,
    wout_sem,
    ns_sem,
    nr_sem,
    ts_sem,
    tr_sem,
    gs_sem,
    gr_sem,
):
    n_col, n_ta, cap, hh, ww, width, bot = dims
    n_dev = n_col * n_ta
    extra = cap - FR
    wp = 16
    rf = hh * wp
    stride = (hh + 2) * wp
    lead = 8
    n_local = float(FR * hh * ww)
    n_total = n_local * n_dev
    chunks = width // 256
    col, ta = lax.axis_index("col"), lax.axis_index("ta")
    me = col * n_ta + ta
    odd = lax.rem(ta, 2)
    sib = (col, ta + 1 - 2 * odd)
    nxt = (col, lax.rem(ta + 1, n_ta))
    prv = (col, lax.rem(ta + n_ta - 1, n_ta))

    def peer(k):
        other = lax.rem(me + k, n_dev)
        return (lax.div(other, n_ta), lax.rem(other, n_ta))

    own_cp = pltpu.make_async_copy(frames, pool.at[pl.ds(0, cap)], in_sem.at[0])
    own_cp.start()
    barrier = pltpu.get_barrier_semaphore()

    def greet(k, carry):
        pl.semaphore_signal(barrier, inc=1, device_id=peer(k), device_id_type=MESH)
        return carry

    loop(1, n_dev, greet)

    live_row = (lax.broadcasted_iota(jnp.int32, (wp, 1), 0) < ww).astype(F32)

    def masked(values):
        c = values.shape[-1]
        return (values.reshape(-1, wp, c) * live_row[None]).reshape(-1, c)

    def rowsum(values):
        return jnp.sum(values.reshape(-1, wp, values.shape[-1]), axis=0)

    def live_total(acc):
        return jnp.sum(acc * live_row, axis=0, keepdims=True)

    def zero_tile(f, carry):
        a0[f] = jnp.zeros((hh, wp, width), BF16)
        pbuf[f] = jnp.zeros((hh, wp, width), BF16)
        return carry

    loop(0, FR, zero_tile)
    for ref in (cbuf.at[0], cbuf.at[1], dbuf):

        def zero_conv(i, carry, ref=ref):
            for h in range(2):
                ref[h, pl.ds(pl.multiple_of(i * 64, 64), 64)] = jnp.zeros((64, 128), F32)
            return carry

        loop(0, ref.shape[1] // 64, zero_conv)

    pl.semaphore_wait(barrier, n_dev - 1)

    def swap_in(src):
        cp = pltpu.make_async_remote_copy(
            src_ref=src.at[pl.ds((1 - odd) * FR, extra)],
            dst_ref=pool.at[pl.ds(cap, extra)],
            send_sem=rem_sem.at[0],
            recv_sem=rem_sem.at[1],
            device_id=sib,
            device_id_type=MESH,
        )
        cp.start()
        return cp

    first_held = held[col, ta - odd]

    def gather_into(dst):
        def pick_frame(j, carry):
            own = jnp.where(odd == 0, j, j + FR - first_held)
            far = jnp.where(odd == 0, j - first_held, j)
            mine = jnp.where(odd == 0, j < first_held, own >= 0)
            pick = jnp.where(mine, jnp.clip(own, 0, cap - 1), cap + jnp.clip(far, 0, extra - 1))
            dst[j, :, 0:ww, :] = pool[pick]
            return carry

        loop(0, FR, pick_frame)

    cp = swap_in(frames)
    own_cp.wait()
    cp.wait()
    gather_into(a0)
    own_cp = pltpu.make_async_copy(gout, pool.at[pl.ds(0, cap)], in_sem.at[0])
    own_cp.start()

    def along_ta(k):
        return (col, lax.rem(ta + k, n_ta))

    def along_col(k):
        return (lax.rem(col + k, n_col), ta)

    stages = {
        "all": (nbuf, ns_sem, nr_sem, n_dev, me, peer),
        "ta": (tbuf, ts_sem, tr_sem, n_ta, ta, along_ta),
        "col": (gbuf, gs_sem, gr_sem, n_col, col, along_col),
    }
    used = {"all": 0, "ta": 0, "col": 0}

    def exchange(name, values, between=None):
        buf, ssem, rsem, size, mine, who = stages[name]
        par = used[name] % 2
        used[name] += 1
        buf[par, mine] = values

        def send(k, carry):
            pltpu.make_async_remote_copy(
                src_ref=buf.at[par, mine],
                dst_ref=buf.at[par, mine],
                send_sem=ssem.at[par],
                recv_sem=rsem.at[par],
                device_id=who(k),
                device_id_type=MESH,
            ).start()
            return carry

        loop(1, size, send)
        if between is not None:
            between()
        part = buf.at[par, pl.ds(0, size - 1)]
        pltpu.make_async_copy(part, part, rsem.at[par]).wait()
        pltpu.make_async_copy(part, part, ssem.at[par]).wait()
        return buf[par]

    def merge(name, mean_l, m2_l, per, size, between=None):
        got = exchange(name, jnp.concatenate([mean_l, m2_l], axis=0), between)
        total = jnp.sum(got, axis=0)
        mean = total[0:1] * (1.0 / size)
        dev = got - mean[None]
        spread = jnp.sum(dev * dev, axis=0)[0:1]
        return mean, total[1:2] + per * spread

    def moments(mean_l, m2_l, wide, between=None):
        if wide:
            mean, m2 = merge("ta", mean_l, m2_l, n_local, n_ta, between)
            mean, m2 = merge("col", mean, m2, n_local * n_ta, n_col)
        else:
            mean, m2 = merge("all", mean_l, m2_l, n_local, n_dev, between)
        return mean, lax.rsqrt(m2 * (1.0 / n_total) + EPS)

    def sums(s0, s1, wide, between=None):
        total = jnp.concatenate([s0, s1], axis=0)
        if wide:
            total = jnp.sum(exchange("ta", total, between), axis=0)
            total = jnp.sum(exchange("col", total), axis=0)
        else:
            total = jnp.sum(exchange("all", total, between), axis=0)
        return total[0:1], total[1:2]

    def rows(f):
        return pl.ds(pl.multiple_of(f * rf, rf), rf)

    def ld_h(f):
        return jnp.concatenate([hbuf[0, rows(f)], hbuf[1, rows(f)]], axis=1)

    def st_h(f, values):
        hbuf[0, rows(f)] = values[:, :128]
        hbuf[1, rows(f)] = values[:, 128:]

    def conv_rows(slot):
        return pl.ds(pl.multiple_of(lead + slot * stride + wp, 8), rf)

    def st_conv(ref, slot, values):
        ref[0, conv_rows(slot)] = values[:, :128]
        ref[1, conv_rows(slot)] = values[:, 128:]

    def local_m2(mean_l):
        sacc[0:wp, 0:bot] = jnp.zeros((wp, bot), F32)

        def to_m2(f, carry):
            d = ld_h(f) - mean_l
            sacc[0:wp, 0:bot] += rowsum(d * d)
            return carry

        loop(0, FR, to_m2)
        return live_total(sacc[0:wp, 0:bot])

    def conv_frame(src, wrow, f, flip):
        def half(h, carry):
            wts = []
            w_all = prm[h]
            for dt in range(3):
                scale = None
                if dt == 0:
                    scale = okmask[0, f]
                if dt == 2:
                    scale = okmask[1, f]
                for sp in range(9):
                    idx = dt * 9 + sp
                    row = w_all[26 - idx : 27 - idx] if flip else w_all[idx : idx + 1]
                    if scale is not None:
                        row = row * scale
                    wts.append(jnp.broadcast_to(row, (8, 128)))
            out = []
            for y in range(hh):
                for s in range(2):
                    acc = [None, None, None]
                    for dt in range(3):
                        for dy in range(3):
                            for dx in range(3):
                                off = lead + dt * stride + (y + dy) * wp + dx - 1 + s * 8
                                v = src[h, pl.ds(f * stride + off, 8)]
                                term = v * wts[dt * 9 + dy * 3 + dx]
                                acc[dx] = term if acc[dx] is None else acc[dx] + term
                    val = acc[0] + acc[1] + acc[2]
                    hbuf[h, pl.ds(pl.multiple_of(f * rf + y * wp + s * 8, 8), 8)] = val
            return carry

        loop(0, 2, half)

    def load_taps(b):
        k = taps[b].astype(F32)
        prm[0, 0:27] = k[:, :128]
        prm[1, 0:27] = k[:, 128:]

    def send_halos(ref, which):
        cps = []
        for i, (slot, land, dev) in enumerate(((1, FR + 1, prv), (FR, 0, nxt))):
            cp = pltpu.make_async_remote_copy(
                src_ref=ref.at[:, pl.ds(lead + slot * stride + wp, rf)],
                dst_ref=ref.at[:, pl.ds(lead + land * stride + wp, rf)],
                send_sem=halo_sem.at[which, i, 0],
                recv_sem=halo_sem.at[which, i, 1],
                device_id=dev,
                device_id_type=MESH,
            )
            cp.start()
            cps.append(cp)
        return cps

    def edge_first(step):
        step(0, 0)
        step(FR - 1, 0)

    def chunk(c):
        return pl.ds(c * 256, 256)

    def flat(ref, f, c):
        return ref[f, :, :, chunk(c)].reshape(rf, 256)

    def put(ref, f, c, values):
        ref[f, :, :, chunk(c)] = values.reshape(hh, wp, 256)

    def first_mm(src, b):
        sacc[0:wp, 0:bot] = jnp.zeros((wp, bot), F32)

        def to_h1(f, carry):
            h1 = dot_nn(src[f].reshape(rf, width), w1[b])
            st_h(f, h1)
            sacc[0:wp, 0:bot] += rowsum(h1)
            return carry

        loop(0, FR, to_h1)
        mean_l = live_total(sacc[0:wp, 0:bot]) * (1.0 / n_local)
        return mean_l, local_m2(mean_l)

    inv1, inv2, mean3, inv3 = {}, {}, {}, {}

    def vec(ref, b, j):
        return ref[b].astype(F32)[j : j + 1]

    def wvec(ref, b):
        return ref[...].astype(F32)[b : b + 1]

    def get_gout():
        own_cp.wait()

    def block_forward(b, src, after_first):
        mean_l, m2_l = first_mm(src, b)
        mean, inv = moments(mean_l, m2_l, False, None)
        inv1[b] = inv
        after_first()
        g, bb = vec(ngain, b, 0), vec(nbias, b, 0)

        def to_h2(f, carry):
            xhat = (ld_h(f) - mean) * inv
            x1b[b, rows(f)] = xhat.astype(BF16)
            u1 = masked(silu(xhat * g + bb)).astype(BF16)
            h2 = dot_nn(u1, w2[b]).astype(BF16).astype(F32)
            st_conv(cbuf.at[b], f + 1, h2)
            return carry

        edge_first(to_h2)
        cps = send_halos(cbuf.at[b], b)
        loop(1, FR - 1, to_h2)
        load_taps(b)

        def conv_step(f, carry):
            conv_frame(cbuf.at[b], None, f, False)
            return carry

        loop(1, FR - 1, conv_step)
        for cp in cps:
            cp.wait()
        conv_step(0, 0)
        conv_step(FR - 1, 0)
        sacc[0:wp, 0:bot] = jnp.zeros((wp, bot), F32)

        def dw_sum(f, carry):
            sacc[0:wp, 0:bot] += rowsum(ld_h(f))
            return carry

        loop(0, FR, dw_sum)
        mean_l = live_total(sacc[0:wp, 0:bot]) * (1.0 / n_local)
        m2_l = local_m2(mean_l)
        mean, inv = moments(mean_l, m2_l, False, None)
        inv2[b] = inv
        g, bb = vec(ngain, b, 1), vec(nbias, b, 1)
        sacc[0:wp, 0:bot] = jnp.zeros((wp, bot), F32)

        def to_u2(f, carry):
            xhat = (ld_h(f) - mean) * inv
            x2b[b, rows(f)] = xhat.astype(BF16)
            u2 = masked(silu(xhat * g + bb))
            u2b[b, rows(f)] = u2.astype(BF16)
            sacc[0:wp, 0:bot] += rowsum(u2)
            return carry

        loop(0, FR, to_u2)
        u_mean = live_total(sacc[0:wp, 0:bot]) * (1.0 / n_local)
        pivot = dot_nn(jnp.broadcast_to(u_mean, (16, bot)).astype(BF16), w3[b])[0:1]
        sacc[...] = jnp.zeros(sacc.shape, F32)

        def h3_stats(f, carry):
            left = u2b[b, rows(f)]
            for c in range(chunks):
                h3 = dot_nn(left, w3[b, :, chunk(c)]) - pivot[:, c * 256 : c * 256 + 256]
                sacc[0:wp, chunk(c)] += rowsum(h3)
                sacc[wp : 2 * wp, chunk(c)] += rowsum(h3 * h3)
            return carry

        loop(0, FR, h3_stats)
        s1 = live_total(sacc[0:wp]) * (1.0 / n_local)
        s2 = live_total(sacc[wp : 2 * wp])
        mean3[b], inv3[b] = moments(pivot + s1, s2 - n_local * s1 * s1, True, None)

    def second_in():
        nonlocal cp2
        cp2 = swap_in(gout)

    cp2 = None
    block_forward(0, a0, second_in)

    g3, b3 = wvec(wgain, 0), wvec(wbias, 0)
    sc, sh = g3 * inv3[0], b3 - mean3[0] * g3 * inv3[0]

    def to_a1(f, carry):
        left = u2b[0, rows(f)]
        for c in range(chunks):
            s = slice(c * 256, c * 256 + 256)
            h3 = dot_nn(left, w3[0, :, chunk(c)])
            pre = flat(a0, f, c).astype(F32) + (h3 * sc[:, s] + sh[:, s])
            put(a1, f, c, silu(pre).astype(BF16))
        return carry

    loop(0, FR, to_a1)

    def none():
        pass

    own_cp.wait()
    cp2.wait()
    gather_into(pbuf)
    block_forward(1, a1, none)

    g3, b3 = wvec(wgain, 1), wvec(wbias, 1)
    nxhat = mean3[1] * inv3[1]
    sacc[...] = jnp.zeros(sacc.shape, F32)

    def out_copy(f, dst):
        slot = lax.rem(f, 2)
        return pltpu.make_async_copy(ost.at[slot], dst.at[f], out_sem.at[slot])

    def turn(f, carry):
        @pl.when(f >= 2)
        def _():
            out_copy(f - 2, a2w).wait()

        slot = lax.rem(f, 2)
        left = u2b[1, rows(f)]
        for c in range(chunks):
            s = slice(c * 256, c * 256 + 256)
            h3 = dot_nn(left, w3[1, :, chunk(c)])
            xhat = h3 * inv3[1][:, s] - nxhat[:, s]
            pre = flat(a1, f, c).astype(F32) + (xhat * g3[:, s] + b3[:, s])
            act, slope = silu_and_slope(pre)
            ost[slot, :, :, chunk(c)] = act.astype(BF16).reshape(hh, wp, 256)[:, 0:ww]
            grad = flat(pbuf, f, c).astype(F32) * slope
            put(pbuf, f, c, grad.astype(BF16))
            sacc[0:wp, chunk(c)] += rowsum(grad)
            sacc[wp : 2 * wp, chunk(c)] += rowsum(grad * xhat)
        out_copy(f, a2w).start()
        return carry

    loop(0, FR, turn)
    out_copy(FR - 2, a2w).wait()
    out_copy(FR - 1, a2w).wait()

    def swap_out(src, dst, i):
        cp = pltpu.make_async_remote_copy(
            src_ref=src.at[pl.ds((1 - odd) * (FR - extra), extra)],
            dst_ref=dst,
            send_sem=rem_sem.at[2 + i],
            recv_sem=rem_sem.at[4 + i],
            device_id=sib,
            device_id_type=MESH,
        )
        cp.start()
        return cp

    ret_a = swap_out(a2w, a2r, 0)
    sum_p, sum_px = live_total(sacc[0:wp]), live_total(sacc[wp : 2 * wp])

    def put_out(src, dst, i):
        cp = pltpu.make_async_copy(src, dst, wout_sem.at[i])
        cp.start()
        return cp

    pending = {}

    def block_backward(b):
        nonlocal sum_p, sum_px
        act_src = a1 if b else a0
        s0, s1 = sums(sum_p, sum_px, True, None)
        o_wb[b : b + 1] = s0
        o_wg[b : b + 1] = s1
        k3 = wvec(wgain, b) * inv3[b]
        c0, c1 = s0 * (1.0 / n_total), s1 * (1.0 / n_total)
        ch = k3 * c1 * inv3[b]
        cc = ch * mean3[b] - k3 * c0
        g2, b2 = vec(ngain, b, 1), vec(nbias, b, 1)
        sacc[0 : 2 * wp, 0:bot] = jnp.zeros((2 * wp, bot), F32)
        if 3 in pending:
            pending.pop(3).wait()
        wacc[0] = jnp.zeros((bot, width), F32)

        def to_z2(f, carry):
            left = u2b[b, rows(f)]
            for c in range(chunks):
                s = slice(c * 256, c * 256 + 256)
                h3 = dot_nn(left, w3[b, :, chunk(c)])
                dh3 = flat(pbuf, f, c).astype(F32) * k3[:, s] - h3 * ch[:, s] + cc[:, s]
                tile[:, chunk(c)] = dh3.astype(BF16)
            du2 = dot_nt(tile[...], w3[b])
            for c in range(chunks):
                wacc[0, :, chunk(c)] += dot_tn(left, tile[:, chunk(c)])
            xhat = x2b[b, rows(f)].astype(F32)
            _, slope = silu_and_slope(xhat * g2 + b2)
            z = du2 * slope
            st_h(f, z)
            sacc[0:wp, 0:bot] += rowsum(z)
            sacc[wp : 2 * wp, 0:bot] += rowsum(z * xhat)
            return carry

        loop(0, FR, to_z2)
        pending[3] = put_out(wacc.at[0], o_w3.at[b], 0)
        s0, s1 = sums(live_total(sacc[0:wp, 0:bot]), live_total(sacc[wp : 2 * wp, 0:bot]), False)
        o_nb[b, 1:2] = s0
        o_ng[b, 1:2] = s1
        k2 = g2 * inv2[b]
        c0, c1 = s0 * (1.0 / n_total), s1 * (1.0 / n_total)

        def to_ddw(f, carry):
            xhat = x2b[b, rows(f)].astype(F32)
            st_conv(dbuf, f + 1, masked(k2 * (ld_h(f) - c0 - xhat * c1)))
            return carry

        edge_first(to_ddw)
        cps = send_halos(dbuf, 2)
        loop(1, FR - 1, to_ddw)
        load_taps(b)

        def conv_back(f, carry):
            conv_frame(dbuf, None, f, True)
            return carry

        loop(1, FR - 1, conv_back)
        for cp in cps:
            cp.wait()
        conv_back(0, 0)
        conv_back(FR - 1, 0)
        g1, b1 = vec(ngain, b, 0), vec(nbias, b, 0)
        sacc[0 : 2 * wp, 0:bot] = jnp.zeros((2 * wp, bot), F32)
        if 2 in pending:
            pending.pop(2).wait()
        w2acc[...] = jnp.zeros((bot, bot), F32)

        def to_z1(f, carry):
            dh2 = ld_h(f).astype(BF16)
            xhat = x1b[b, rows(f)].astype(F32)
            act, slope = silu_and_slope(xhat * g1 + b1)
            u1 = masked(act).astype(BF16)
            w2acc[...] += dot_tn(u1, dh2)
            z = dot_nt(dh2, w2[b]) * slope
            st_h(f, z)
            sacc[0:wp, 0:bot] += rowsum(z)
            sacc[wp : 2 * wp, 0:bot] += rowsum(z * xhat)
            return carry

        loop(0, FR, to_z1)
        pending[2] = put_out(w2acc, o_w2.at[b], 1)

        def tap_grads():
            kacc[...] = jnp.zeros(kacc.shape, F32)

            def frame(f, carry):
                def half(h, carry2):
                    for dt in range(3):
                        acc = [None] * 9
                        for y in range(hh):
                            for s in range(2):
                                base = lead + (y + 1) * wp + s * 8
                                gv = dbuf[h, pl.ds(pl.multiple_of(f * stride, 8) + stride + base, 8)]
                                for dy in range(3):
                                    for dx in range(3):
                                        off = lead + dt * stride + (y + dy) * wp + dx - 1 + s * 8
                                        v = cbuf[b, h, pl.ds(f * stride + off, 8)] * gv
                                        i = dy * 3 + dx
                                        acc[i] = v if acc[i] is None else acc[i] + v
                        for i in range(9):
                            val = acc[i]
                            if dt == 0:
                                val = val * okmask[0, f]
                            if dt == 2:
                                val = val * okmask[1, f]
                            kacc[h, dt * 9 + i] += val
                    return carry2

                loop(0, 2, half)
                return carry

            loop(0, FR, frame)
            for h in range(2):
                o_k[b, :, h * 128 : h * 128 + 128] = jnp.sum(kacc[h], axis=1)

        s0, s1 = sums(
            live_total(sacc[0:wp, 0:bot]), live_total(sacc[wp : 2 * wp, 0:bot]), False, tap_grads
        )
        o_nb[b, 0:1] = s0
        o_ng[b, 0:1] = s1
        k1 = g1 * inv1[b]
        c0, c1 = s0 * (1.0 / n_total), s1 * (1.0 / n_total)

        def to_dh1(f, carry):
            xhat = x1b[b, rows(f)].astype(F32)
            dhb[rows(f)] = masked(k1 * (ld_h(f) - c0 - xhat * c1)).astype(BF16)
            return carry

        loop(0, FR, to_dh1)

        def w1_grad():
            if 1 in pending:
                pending.pop(1).wait()
            wacc[1] = jnp.zeros((bot, width), F32)

            def to_w1(f, carry):
                left = dhb[rows(f)]
                for c in range(chunks):
                    wacc[1, :, chunk(c)] += dot_tn(left, flat(act_src, f, c))
                return carry

            loop(0, FR, to_w1)
            pending[1] = put_out(wacc.at[1], o_w1t.at[b], 2)

        return w1_grad

    w1_grad = block_backward(1)
    g3, b3 = wvec(wgain, 0), wvec(wbias, 0)
    nxhat = mean3[0] * inv3[0]
    sacc[...] = jnp.zeros(sacc.shape, F32)

    def middle(f, carry):
        left = u2b[0, rows(f)]
        dh1 = dhb[rows(f)]
        for c in range(chunks):
            s = slice(c * 256, c * 256 + 256)
            grad = dot_nt(dh1, w1[1, chunk(c), :]) + flat(pbuf, f, c).astype(F32)
            h3 = dot_nn(left, w3[0, :, chunk(c)])
            xhat = h3 * inv3[0][:, s] - nxhat[:, s]
            pre = flat(a0, f, c).astype(F32) + (xhat * g3[:, s] + b3[:, s])
            _, slope = silu_and_slope(pre)
            grad = grad * slope
            put(pbuf, f, c, grad.astype(BF16))
            sacc[0:wp, chunk(c)] += rowsum(grad)
            sacc[wp : 2 * wp, chunk(c)] += rowsum(grad * xhat)
        return carry

    loop(0, FR, middle)
    sum_p, sum_px = live_total(sacc[0:wp]), live_total(sacc[wp : 2 * wp])
    w1_grad()
    w1_grad = block_backward(0)

    def last(f, carry):
        @pl.when(f >= 2)
        def _():
            out_copy(f - 2, gw).wait()

        slot = lax.rem(f, 2)
        dh1 = dhb[rows(f)]
        for c in range(chunks):
            grad = dot_nt(dh1, w1[0, chunk(c), :]) + flat(pbuf, f, c).astype(F32)
            ost[slot, :, :, chunk(c)] = grad.astype(BF16).reshape(hh, wp, 256)[:, 0:ww]
        out_copy(f, gw).start()
        return carry

    loop(0, FR, last)
    out_copy(FR - 2, gw).wait()
    out_copy(FR - 1, gw).wait()
    ret_g = swap_out(gw, gr, 1)
    w1_grad()
    for i in (1, 2, 3):
        pending.pop(i).wait()
    ret_a.wait()
    ret_g.wait()


def run_main(dims, held, okmask, frames, gout, w1, w2, w3, taps, ngain, nbias, wgain, wbias):
    n_col, n_ta, cap, hh, ww, width, bot = dims
    n_dev = n_col * n_ta
    extra = cap - FR
    rf = hh * 16
    conv_rows = 8 + (FR + 2) * (hh + 2) * 16 + 8
    conv_rows = -(-conv_rows // 64) * 64
    sds = jax.ShapeDtypeStruct
    outs = (
        sds((FR, hh, ww, width), BF16),
        sds((extra, hh, ww, width), BF16),
        sds((FR, hh, ww, width), BF16),
        sds((extra, hh, ww, width), BF16),
        sds((2, bot, width), F32),
        sds((2, bot, bot), F32),
        sds((2, bot, width), F32),
        sds((2, 27, bot), F32),
        sds((2, 2, bot), F32),
        sds((2, 2, bot), F32),
        sds((2, width), F32),
        sds((2, width), F32),
    )
    vm = pltpu.VMEM
    dma = pltpu.SemaphoreType.DMA
    scratch = [
        vm((cap + extra, hh, ww, width), BF16),
        vm((FR, hh, 16, width), BF16),
        vm((FR, hh, 16, width), BF16),
        vm((FR, hh, 16, width), BF16),
        vm((rf, width), BF16),
        vm((2, hh, ww, width), BF16),
        vm((2, FR * rf, bot), BF16),
        vm((2, FR * rf, 128), F32),
        vm((2, FR * rf, bot), BF16),
        vm((2, FR * rf, bot), BF16),
        vm((2, 2, conv_rows, 128), F32),
        vm((2, conv_rows, 128), F32),
        vm((FR * rf, bot), BF16),
        vm((2, bot, width), F32),
        vm((bot, bot), F32),
        vm((2, 27, 8, 128), F32),
        vm((2, n_dev, 2, bot), F32),
        vm((2, n_ta, 2, width), F32),
        vm((2, n_col, 2, width), F32),
        vm((32, width), F32),
        vm((2, 32, 128), F32),
        dma((1,)),
        dma((6,)),
        dma((3, 2, 2)),
        dma((2,)),
        dma((3,)),
        dma((2,)),
        dma((2,)),
        dma((2,)),
        dma((2,)),
        dma((2,)),
        dma((2,)),
    ]
    return pl.pallas_call(
        functools.partial(main_kernel, dims),
        out_shape=outs,
        in_specs=[SM, SM, ANY, ANY] + [VM] * 8,
        out_specs=(ANY,) * 7 + (VM,) * 5,
        scratch_shapes=scratch,
        compiler_params=pltpu.CompilerParams(
            collective_id=0, has_side_effects=True, vmem_limit_bytes=66_000_000
        ),
        name="blocks",
    )(held, okmask, frames, gout, w1, w2, w3, taps, ngain, nbias, wgain, wbias)


def place_kernel(dims, where, a2w, a2r, gw, gr, out, grad, zero, sem):
    cap = dims[2]
    extra = cap - FR
    zero[...] = jnp.zeros(zero.shape, BF16)
    odd, first = where[0], where[1]
    live = jnp.where(odd == 0, first, 2 * FR - first)

    def each(j, act):
        pos = jnp.where(odd == 0, j, first + j)
        mine = jnp.where(odd == 0, pos < FR, pos >= FR)
        own = jnp.where(odd == 0, pos, pos - FR)
        far = jnp.where(odd == 0, pos - FR, pos - (FR - extra))
        for i, (work, back, dst) in enumerate(((a2w, a2r, out), (gw, gr, grad))):

            @pl.when((j < live) & mine)
            def _():
                act(pltpu.make_async_copy(work.at[own], dst.at[j], sem.at[i]))

            @pl.when((j < live) & jnp.logical_not(mine))
            def _():
                act(pltpu.make_async_copy(back.at[far], dst.at[j], sem.at[i]))

            @pl.when(j >= live)
            def _():
                act(pltpu.make_async_copy(zero, dst.at[j], sem.at[i]))

    def start(j, carry):
        each(j, lambda cp: cp.start())
        return carry

    loop(0, cap, start)
    pltpu.make_async_copy(out, out, sem.at[0]).wait()
    pltpu.make_async_copy(grad, grad, sem.at[1]).wait()


def place(dims, where, a2w, a2r, gw, gr):
    n_col, n_ta, cap, hh, ww, width, bot = dims
    sds = jax.ShapeDtypeStruct
    return pl.pallas_call(
        functools.partial(place_kernel, dims),
        out_shape=(sds((cap, hh, ww, width), BF16),) * 2,
        in_specs=[SM] + [ANY] * 4,
        out_specs=(ANY, ANY),
        scratch_shapes=[pltpu.VMEM((hh, ww, width), BF16), pltpu.SemaphoreType.DMA((2,))],
        name="place",
    )(where, a2w, a2r, gw, gr)


def body(
    n_col,
    n_ta,
    frames,
    out_grad,
    held,
    clip_stride,
    w_reduce,
    w_mid,
    depth_kernel,
    w_expand,
    narrow_gain,
    narrow_bias,
    wide_gain,
    wide_bias,
):
    cap, hh, ww, width = frames.shape
    dims = (n_col, n_ta, cap, hh, ww, width, w_mid.shape[1])
    col, ta = lax.axis_index("col"), lax.axis_index("ta")
    odd = lax.rem(ta, 2)
    lengths = 8 // lax.dynamic_index_in_dim(clip_stride, col, 0, keepdims=False)
    clips = lengths.shape[0]
    before = jnp.arange(clips)[:, None] < jnp.arange(clips)[None, :]
    starts = jnp.sum(jnp.where(before, lengths[:, None], 0), axis=0)
    ids = ta * FR + jnp.arange(FR + 1)
    begins = jnp.any(starts[None, :] == ids[:, None], axis=1) | (ids >= n_ta * FR)
    ok = jnp.logical_not(begins).astype(F32)
    okmask = jnp.stack([ok[:-1], ok[1:]])
    (a2w, a2r, gw, gr, g_w1t, g_w2, g_w3, g_k, g_ng, g_nb, g_wg, g_wb) = run_main(
        dims,
        held,
        okmask,
        frames,
        out_grad,
        w_reduce,
        w_mid,
        w_expand,
        depth_kernel,
        narrow_gain,
        narrow_bias,
        wide_gain,
        wide_bias,
    )
    where = jnp.stack([odd, held[col, ta - odd]]).astype(jnp.int32)
    out, grad = place(dims, where, a2w, a2r, gw, gr)
    g_w1t, g_w2, g_w3, g_k = lax.psum((g_w1t, g_w2, g_w3, g_k), ("col", "ta"))
    return (
        out,
        grad,
        jnp.swapaxes(g_w1t, 1, 2),
        g_w2,
        g_k,
        g_w3,
        g_ng,
        g_nb,
        g_wg,
        g_wb,
    )


def solution(mesh):
    split = P(("col", "ta"), None, None, None)
    return jax.shard_map(
        functools.partial(body, mesh.shape["col"], mesh.shape["ta"]),
        mesh=mesh,
        in_specs=(split, split) + (P(),) * 10,
        out_specs=(split, split) + (P(),) * 8,
        check_vma=False,
    )
```

time: 1650 us -> 860 us (0.52)
  the two profiles are of different devices: /device:TPU:0 before, /device:TPU:31 now
where the time goes in v1:
time: 860 us; the launch traced here: 856 us
  Pallas kernels  789 us (92%)
  blocking collectives  38.3 us (4%)
  between operations  14.2 us (2%)
  local copies, waits for them, and re-layouts  10.9 us (1%)
    pallas_call x1, Pallas kernels, place(): pl.pallas_call(functools.partial(place_kernel, dims), out_shape=(sds((cap...  585 us
    pallas_call x1, Pallas kernels, run_main(): pl.pallas_call(functools.partial(main_kernel, dims), out_shape=outs, in_s...  204 us
    psum x1, blocking collectives, body(): g_w1t, g_w2, g_w3, g_k = lax.psum((g_w1t, g_w2, g_w3, g_k), ('col', 'ta'))  38.3 us
  transfers between devices with their start and end apart: 1, of which 0 were waited for; matrix products, arithmetic and copies ran while one was open for 0% of the time, Pallas kernels for 68%

profile of v1, /device:TPU:31, one launch (start us, length us, event | category | flops | bytes accessed | tf_op | source)
XLA Modules:
  0.0 855.7 jit_solution(7041990096563668311)
XLA Ops:
  7.2 0.0 all-reduce.3.cloned.1.call-start
  7.2 0.8 bitcast_select_fusion
  8.0 0.1 select_reduce_fusion
  8.1 0.2 compare_reduce_fusion
  8.3 0.1 slice_bitcast_fusion.1
  8.4 1.4 copy.25.taps
  9.8 0.6 pad_maximum_fusion.okmask
  10.3 203.8 %blocks.1 = (bf16[12,14,14,1024]{3,2,1,0:T(8,128)(2,1)}, bf16[9,14,14,1024]{3,2,1,0:T(8,128)(2,1)}, bf16[12,14,14,1024]{3,2,1,0:T(8,128)(2,1)}, bf16[9,14,14,102...) custom-call(s32[4,8]{1,0:T(4,128)} %held.1, ...), custom_call_target="tpu_custom_call" | custom-call | tf_op jit(solution)/shard_map/blocks/pallas_call | solution.py:788
  214.2 0.0 copy-start.2
  214.2 0.0 all-reduce.3.cloned.1.call-update
  214.2 1.3 dynamic_slice.7
  215.5 0.0 copy-done.2
  215.5 38.3 %psum.30 = f32[2,27,256]{2,1,0:T(8,128)S(1)} all-reduce(f32[2,27,256]{2,1,0:T(8,128)S(1)} %copy-done.2), channel_id=1, replica_groups=mesh['col'=4,'ta'=8] {'col','ta'}, use_global_device_ids=true, to_apply=%region_4.5 | all-reduce | flops 13824 | bytes 110592 | tf_op jit(solution)/shard_map/psum | solution.py:894
  253.8 0.7 copy.27
  254.5 1.2 pad_add_fusion.where
  255.7 585.5 %place.1 = (bf16[21,14,14,1024]{3,2,1,0:T(8,128)(2,1)}, bf16[21,14,14,1024]{3,2,1,0:T(8,128)(2,1)}) custom-call(s32[2]{0:T(128)} %pad_add_fusion.where, bf16[12,14,14,1024]{3,2,1,0:T(8,128)(2,1)} %get-tuple-element.24.a2w, bf16[9,14,14,1024]{3,2,1,0:T(8,128)(2,1)} %get-tuple-element.25.a2r, bf16[12,14,14,1024]{3,2,1,0:T(8,128)(2,1)} %get-tuple-element.26.gw, ...), custom_call_target="tpu_custom_call" | custom-call | tf_op jit(solution)/shard_map/place/pallas_call | solution.py:839
  841.2 0.0 all-reduce.3.cloned.1.call-done
  841.2 0.0 copy-start.1
  841.2 0.0 copy-start
  841.2 0.0 copy-start.6
  841.2 0.0 copy-start.5
  841.2 0.0 copy-start.4
  841.3 0.0 copy-start.3
  841.3 3.0 copy.26
  844.3 0.0 copy-done.1
  844.3 0.8 copy.37
  845.1 0.0 copy-done
  845.1 1.3 copy.38
  846.4 0.6 copy.39
  847.0 0.6 copy.40
  847.6 0.6 copy.41
  848.2 0.6 copy.42
  (6 shorter events, 0.0 us)
Async XLA Ops:
  7.2 834.0 %all-reduce.3.cloned.1.call-start = ((), (), s32[]{:S(2)}) async-start(), calls=%async_computation | async-start | bytes 9437184 | tf_op jit(solution)/shard_map/psum | solution.py:894
  214.2 1.3 copy-start.2
  841.2 3.1 copy-start.1
  841.2 3.9 copy-start
  841.2 5.2 copy-start.6
  841.2 5.8 copy-start.5
  841.2 6.4 copy-start.4
  841.3 7.0 copy-start.3
Sparse Core Ops, SparseCore 0:
  214.3 142.8 all-reduce.2

commit v2 on v1

--- a/solution.py
+++ b/solution.py
@@ -64,10 +64,8 @@
     a2r,
     gw,
     gr,
-    o_w1t,
-    o_w2,
-    o_w3,
-    o_k,
+    o_pa,
+    o_pb,
     o_ng,
     o_nb,
     o_wg,
@@ -84,20 +82,23 @@
     x2b,
     cbuf,
     dbuf,
-    dhb,
     wacc,
     w2acc,
     kacc,
+    ksum,
     nbuf,
     tbuf,
     gbuf,
     sacc,
     prm,
+    pa_bufs,
+    pb_bufs,
     in_sem,
     rem_sem,
     halo_sem,
     out_sem,
-    wout_sem,
+    pa_sem,
+    pb_sem,
     ns_sem,
     nr_sem,
     ts_sem,
@@ -214,12 +215,13 @@
         buf, ssem, rsem, size, mine, who = stages[name]
         par = used[name] % 2
         used[name] += 1
-        buf[par, mine] = values
+        lanes = pl.ds(0, values.shape[1])
+        buf[par, mine, :, lanes] = values
 
         def send(k, carry):
             pltpu.make_async_remote_copy(
-                src_ref=buf.at[par, mine],
-                dst_ref=buf.at[par, mine],
+                src_ref=buf.at[par, mine, :, lanes],
+                dst_ref=buf.at[par, mine, :, lanes],
                 send_sem=ssem.at[par],
                 recv_sem=rsem.at[par],
                 device_id=who(k),
@@ -230,10 +232,10 @@
         loop(1, size, send)
         if between is not None:
             between()
-        part = buf.at[par, pl.ds(0, size - 1)]
+        part = buf.at[par, pl.ds(0, size - 1), :, lanes]
         pltpu.make_async_copy(part, part, rsem.at[par]).wait()
         pltpu.make_async_copy(part, part, ssem.at[par]).wait()
-        return buf[par]
+        return buf[par, :, :, lanes]
 
     def merge(name, mean_l, m2_l, per, size, between=None):
         got = exchange(name, jnp.concatenate([mean_l, m2_l], axis=0), between)
@@ -244,18 +246,18 @@
         return mean, total[1:2] + per * spread
 
     def moments(mean_l, m2_l, wide, between=None):
-        if wide:
+        if wide or n_dev > 64:
             mean, m2 = merge("ta", mean_l, m2_l, n_local, n_ta, between)
             mean, m2 = merge("col", mean, m2, n_local * n_ta, n_col)
         else:
             mean, m2 = merge("all", mean_l, m2_l, n_local, n_dev, between)
         return mean, lax.rsqrt(m2 * (1.0 / n_total) + EPS)
 
-    def sums(s0, s1, wide, between=None):
+    def sums(s0, s1, wide, between=None, later=None):
         total = jnp.concatenate([s0, s1], axis=0)
-        if wide:
+        if wide or n_dev > 64:
             total = jnp.sum(exchange("ta", total, between), axis=0)
-            total = jnp.sum(exchange("col", total), axis=0)
+            total = jnp.sum(exchange("col", total, later), axis=0)
         else:
             total = jnp.sum(exchange("all", total, between), axis=0)
         return total[0:1], total[1:2]
@@ -354,6 +356,140 @@
     def put(ref, f, c, values):
         ref[f, :, :, chunk(c)] = values.reshape(hh, wp, 256)
 
+    nz = n_ta // 2
+    zpos = lax.div(ta, 2)
+    if n_dev == 32:
+        first = col * nz + zpos
+        levels = [
+            (
+                n_dev // 2,
+                16,
+                first,
+                lambda i: (lax.div(i, nz), 2 * lax.rem(i, nz) + odd),
+            )
+        ]
+    else:
+        levels = [
+            (n_col, 4, col, lambda i: (i, ta)),
+            (nz, 4, zpos, lambda i: (col, 2 * i + odd)),
+        ]
+
+    def package(bufs, sems, dst):
+        send, land, final = bufs[0], bufs[1], bufs[2]
+        halls = bufs[3:]
+
+        def remote(src, to, i, dev):
+            return pltpu.make_async_remote_copy(
+                src_ref=src,
+                dst_ref=to,
+                send_sem=sems.at[2 * i],
+                recv_sem=sems.at[2 * i + 1],
+                device_id=dev,
+                device_id_type=MESH,
+            )
+
+        cp = remote(send.at[1 - odd], land, 0, sib)
+        cp.start()
+        yield
+        cp.wait()
+
+        def add(r, carry):
+            both = send[odd, r].astype(F32) + land[r].astype(F32)
+            send[odd, r] = both.astype(BF16)
+            return carry
+
+        loop(0, 16, add)
+        off, size = 0, 16
+        spans = []
+        for i, (n, m, mine, who) in enumerate(levels):
+            hall = halls[i]
+            size = size // m
+
+            def scatter(k, carry, hall=hall, size=size, off=off, n=n, m=m, mine=mine, who=who, i=i):
+                other = lax.rem(mine + k, n)
+                part = send.at[odd, pl.ds(off + lax.rem(other, m) * size, size)]
+                remote(part, hall.at[mine], 1 + i, who(other)).start()
+                return carry
+
+            loop(1, n, scatter)
+            off = off + lax.rem(mine, m) * size
+            hall[mine] = send[odd, pl.ds(off, size)]
+            yield
+            part = hall.at[pl.ds(0, n - 1)]
+            pltpu.make_async_copy(part, part, sems.at[3 + 2 * i]).wait()
+            pltpu.make_async_copy(part, part, sems.at[2 + 2 * i]).wait()
+            last = i == len(levels) - 1
+
+            def reduce(q, carry, hall=hall, n=n, off=off, last=last):
+                total = jnp.sum(hall[:, q].astype(F32), axis=0).astype(BF16)
+                if last:
+                    final[odd, off + q] = total
+                else:
+                    send[odd, off + q] = total
+                return carry
+
+            loop(0, size, reduce)
+            spans.append((off, size))
+        base = 1 + len(levels)
+        for i in reversed(range(len(levels))):
+            n, m, mine, who = levels[i]
+            off, size = spans[i]
+
+            def spread(k, carry, off=off, size=size, m=m, mine=mine, who=who, i=i):
+                other = lax.div(mine, m) * m + lax.rem(lax.rem(mine, m) + k, m)
+                part = final.at[odd, pl.ds(off, size)]
+                remote(part, part, base + i, who(other)).start()
+                return carry
+
+            loop(1, m, spread)
+            yield
+            part = final.at[odd, pl.ds(0, (m - 1) * size)]
+            pltpu.make_async_copy(part, part, sems.at[2 * (base + i) + 1]).wait()
+            pltpu.make_async_copy(part, part, sems.at[2 * (base + i)]).wait()
+        cp = remote(final.at[odd], final.at[odd], base + len(levels), sib)
+        cp.start()
+        yield
+        cp.wait()
+        cp = pltpu.make_async_copy(final, dst, sems.at[2 * (base + len(levels)) + 2])
+        cp.start()
+        yield
+        cp.wait()
+        yield
+
+    def finish(gen):
+        for _ in gen:
+            pass
+
+    def advance(*gens):
+        for gen in gens:
+            next(gen, None)
+
+    ksum[...] = jnp.zeros(ksum.shape, F32)
+    pa_bufs[0][...] = jnp.zeros(pa_bufs[0].shape, BF16)
+    half_w = width // 2
+
+    def pack_a():
+        def step(r, carry):
+            rr = pl.ds(pl.multiple_of(r * 16, 16), 16)
+            for p in range(2):
+                pa_bufs[0][p, r, :, 0:half_w] = wacc[rr, p * half_w : p * half_w + half_w].astype(BF16)
+                pa_bufs[0][p, r, :, half_w : half_w + 128] = w2acc[rr, p * 128 : p * 128 + 128].astype(BF16)
+            return carry
+
+        loop(0, 16, step)
+        for p in range(2):
+            for r in range(2):
+                pa_bufs[0][p, r, :, half_w + 128 :] = ksum[p, r * 16 : r * 16 + 16].astype(BF16)
+
+    def pack_b():
+        def step(r, carry):
+            rr = pl.ds(pl.multiple_of(r * 16, 16), 16)
+            for p in range(2):
+                pb_bufs[0][p, r] = wacc[rr, p * half_w : p * half_w + half_w].astype(BF16)
+            return carry
+
+        loop(0, 16, step)
+
     def first_mm(src, b):
         sacc[0:wp, 0:bot] = jnp.zeros((wp, bot), F32)
 
@@ -524,17 +660,8 @@
     ret_a = swap_out(a2w, a2r, 0)
     sum_p, sum_px = live_total(sacc[0:wp]), live_total(sacc[wp : 2 * wp])
 
-    def put_out(src, dst, i):
-        cp = pltpu.make_async_copy(src, dst, wout_sem.at[i])
-        cp.start()
-        return cp
-
-    pending = {}
-
-    def block_backward(b):
-        nonlocal sum_p, sum_px
-        act_src = a1 if b else a0
-        s0, s1 = sums(sum_p, sum_px, True, None)
+    def block_backward(b, act_src, windows):
+        s0, s1 = sums(sum_p, sum_px, True, windows[0], windows[1])
         o_wb[b : b + 1] = s0
         o_wg[b : b + 1] = s1
         k3 = wvec(wgain, b) * inv3[b]
@@ -543,9 +670,7 @@
         cc = ch * mean3[b] - k3 * c0
         g2, b2 = vec(ngain, b, 1), vec(nbias, b, 1)
         sacc[0 : 2 * wp, 0:bot] = jnp.zeros((2 * wp, bot), F32)
-        if 3 in pending:
-            pending.pop(3).wait()
-        wacc[0] = jnp.zeros((bot, width), F32)
+        wacc[...] = jnp.zeros((bot, width), F32)
 
         def to_z2(f, carry):
             left = u2b[b, rows(f)]
@@ -556,7 +681,7 @@
                 tile[:, chunk(c)] = dh3.astype(BF16)
             du2 = dot_nt(tile[...], w3[b])
             for c in range(chunks):
-                wacc[0, :, chunk(c)] += dot_tn(left, tile[:, chunk(c)])
+                wacc[:, chunk(c)] += dot_tn(left, tile[:, chunk(c)])
             xhat = x2b[b, rows(f)].astype(F32)
             _, slope = silu_and_slope(xhat * g2 + b2)
             z = du2 * slope
@@ -566,8 +691,9 @@
             return carry
 
         loop(0, FR, to_z2)
-        pending[3] = put_out(wacc.at[0], o_w3.at[b], 0)
-        s0, s1 = sums(live_total(sacc[0:wp, 0:bot]), live_total(sacc[wp : 2 * wp, 0:bot]), False)
+        s0, s1 = sums(
+            live_total(sacc[0:wp, 0:bot]), live_total(sacc[wp : 2 * wp, 0:bot]), False, windows[2]
+        )
         o_nb[b, 1:2] = s0
         o_ng[b, 1:2] = s1
         k2 = g2 * inv2[b]
@@ -588,14 +714,13 @@
             return carry
 
         loop(1, FR - 1, conv_back)
+        windows[3]()
         for cp in cps:
             cp.wait()
         conv_back(0, 0)
         conv_back(FR - 1, 0)
         g1, b1 = vec(ngain, b, 0), vec(nbias, b, 0)
         sacc[0 : 2 * wp, 0:bot] = jnp.zeros((2 * wp, bot), F32)
-        if 2 in pending:
-            pending.pop(2).wait()
         w2acc[...] = jnp.zeros((bot, bot), F32)
 
         def to_z1(f, carry):
@@ -611,8 +736,6 @@
             return carry
 
         loop(0, FR, to_z1)
-        pending[2] = put_out(w2acc, o_w2.at[b], 1)
-
         def tap_grads():
             kacc[...] = jnp.zeros(kacc.shape, F32)
 
@@ -644,7 +767,14 @@
 
             loop(0, FR, frame)
             for h in range(2):
-                o_k[b, :, h * 128 : h * 128 + 128] = jnp.sum(kacc[h], axis=1)
+                ksum[h, 0:27] = jnp.sum(kacc[h], axis=1)
+            windows[4]()
+            pack_a()
+            gen = package(pa_bufs, pa_sem, o_pa.at[b])
+            next(gen)
+            made.append(gen)
+
+        made = []
 
         s0, s1 = sums(
             live_total(sacc[0:wp, 0:bot]), live_total(sacc[wp : 2 * wp, 0:bot]), False, tap_grads
@@ -656,35 +786,39 @@
 
         def to_dh1(f, carry):
             xhat = x1b[b, rows(f)].astype(F32)
-            dhb[rows(f)] = masked(k1 * (ld_h(f) - c0 - xhat * c1)).astype(BF16)
+            x1b[b, rows(f)] = masked(k1 * (ld_h(f) - c0 - xhat * c1)).astype(BF16)
             return carry
 
         loop(0, FR, to_dh1)
 
         def w1_grad():
-            if 1 in pending:
-                pending.pop(1).wait()
-            wacc[1] = jnp.zeros((bot, width), F32)
+            wacc[...] = jnp.zeros((bot, width), F32)
 
             def to_w1(f, carry):
-                left = dhb[rows(f)]
+                left = x1b[b, rows(f)]
                 for c in range(chunks):
-                    wacc[1, :, chunk(c)] += dot_tn(left, flat(act_src, f, c))
+                    wacc[:, chunk(c)] += dot_tn(left, flat(act_src, f, c))
                 return carry
 
             loop(0, FR, to_w1)
-            pending[1] = put_out(wacc.at[1], o_w1t.at[b], 2)
-
-        return w1_grad
-
-    w1_grad = block_backward(1)
+            pack_b()
+            gen = package(pb_bufs, pb_sem, o_pb.at[b])
+            next(gen)
+            return gen
+
+        return w1_grad, made[0]
+
+    def nothing():
+        pass
+
+    w1_grad, gen_a = block_backward(1, a1, [nothing] * 5)
     g3, b3 = wvec(wgain, 0), wvec(wbias, 0)
     nxhat = mean3[0] * inv3[0]
     sacc[...] = jnp.zeros(sacc.shape, F32)
 
     def middle(f, carry):
         left = u2b[0, rows(f)]
-        dh1 = dhb[rows(f)]
+        dh1 = x1b[1, rows(f)]
         for c in range(chunks):
             s = slice(c * 256, c * 256 + 256)
             grad = dot_nt(dh1, w1[1, chunk(c), :]) + flat(pbuf, f, c).astype(F32)
@@ -700,8 +834,22 @@
 
     loop(0, FR, middle)
     sum_p, sum_px = live_total(sacc[0:wp]), live_total(sacc[wp : 2 * wp])
-    w1_grad()
-    w1_grad = block_backward(0)
+    gens = [gen_a]
+
+    def window0():
+        advance(gen_a)
+        gens.append(w1_grad())
+
+    def window1():
+        advance(*gens)
+
+    def window4():
+        for gen in gens:
+            finish(gen)
+
+    w1_last, last_a = block_backward(0, a0, [window0, window1, window1, window1, window4])
+    last_b = w1_last()
+    advance(last_a)
 
     def last(f, carry):
         @pl.when(f >= 2)
@@ -709,20 +857,24 @@
             out_copy(f - 2, gw).wait()
 
         slot = lax.rem(f, 2)
-        dh1 = dhb[rows(f)]
+        dh1 = x1b[0, rows(f)]
         for c in range(chunks):
             grad = dot_nt(dh1, w1[0, chunk(c), :]) + flat(pbuf, f, c).astype(F32)
             ost[slot, :, :, chunk(c)] = grad.astype(BF16).reshape(hh, wp, 256)[:, 0:ww]
         out_copy(f, gw).start()
         return carry
 
-    loop(0, FR, last)
+    half_way = FR // 2
+    loop(0, half_way, last)
+    advance(last_a, last_b)
+    loop(half_way, FR, last)
     out_copy(FR - 2, gw).wait()
     out_copy(FR - 1, gw).wait()
     ret_g = swap_out(gw, gr, 1)
-    w1_grad()
-    for i in (1, 2, 3):
-        pending.pop(i).wait()
+    for _ in range(8):
+        advance(last_a, last_b)
+    finish(last_a)
+    finish(last_b)
     ret_a.wait()
     ret_g.wait()
 
@@ -735,15 +887,24 @@
     conv_rows = 8 + (FR + 2) * (hh + 2) * 16 + 8
     conv_rows = -(-conv_rows // 64) * 64
     sds = jax.ShapeDtypeStruct
+    la, lb = width // 2 + 256, width // 2
+
+    def piece_bufs(lanes):
+        halls = [(16, 1)] if n_dev == 32 else [(n_col, 4), (n_ta // 2, 1)]
+        return [
+            pltpu.VMEM((2, 16, 16, lanes), BF16),
+            pltpu.VMEM((16, 16, lanes), BF16),
+            pltpu.VMEM((2, 16, 16, lanes), BF16),
+        ] + [pltpu.VMEM((n, size, 16, lanes), BF16) for n, size in halls]
+
+    n_sems = 2 * (2 + 2 * (1 if n_dev == 32 else 2)) + 1
     outs = (
         sds((FR, hh, ww, width), BF16),
         sds((extra, hh, ww, width), BF16),
         sds((FR, hh, ww, width), BF16),
         sds((extra, hh, ww, width), BF16),
-        sds((2, bot, width), F32),
-        sds((2, bot, bot), F32),
-        sds((2, bot, width), F32),
-        sds((2, 27, bot), F32),
+        sds((2, 2, 16, 16, la), BF16),
+        sds((2, 2, 16, 16, lb), BF16),
         sds((2, 2, bot), F32),
         sds((2, 2, bot), F32),
         sds((2, width), F32),
@@ -764,20 +925,23 @@
         vm((2, FR * rf, bot), BF16),
         vm((2, 2, conv_rows, 128), F32),
         vm((2, conv_rows, 128), F32),
-        vm((FR * rf, bot), BF16),
-        vm((2, bot, width), F32),
+        vm((bot, width), F32),
         vm((bot, bot), F32),
         vm((2, 27, 8, 128), F32),
-        vm((2, n_dev, 2, bot), F32),
+        vm((2, 32, 128), F32),
+        vm((2, n_dev if n_dev <= 64 else 1, 2, bot), F32),
         vm((2, n_ta, 2, width), F32),
         vm((2, n_col, 2, width), F32),
         vm((32, width), F32),
         vm((2, 32, 128), F32),
+        piece_bufs(la),
+        piece_bufs(lb),
         dma((1,)),
         dma((6,)),
         dma((3, 2, 2)),
         dma((2,)),
-        dma((3,)),
+        dma((n_sems,)),
+        dma((n_sems,)),
         dma((2,)),
         dma((2,)),
         dma((2,)),
@@ -789,61 +953,132 @@
         functools.partial(main_kernel, dims),
         out_shape=outs,
         in_specs=[SM, SM, ANY, ANY] + [VM] * 8,
-        out_specs=(ANY,) * 7 + (VM,) * 5,
+        out_specs=(ANY,) * 6 + (VM,) * 4,
         scratch_shapes=scratch,
         compiler_params=pltpu.CompilerParams(
-            collective_id=0, has_side_effects=True, vmem_limit_bytes=66_000_000
+            collective_id=0, has_side_effects=True, vmem_limit_bytes=66_500_000
         ),
         name="blocks",
     )(held, okmask, frames, gout, w1, w2, w3, taps, ngain, nbias, wgain, wbias)
 
 
-def place_kernel(dims, where, a2w, a2r, gw, gr, out, grad, zero, sem):
-    cap = dims[2]
+def place_kernel(
+    cap,
+    where,
+    a2w,
+    a2r,
+    gw,
+    gr,
+    pa,
+    pb,
+    i_ng,
+    i_nb,
+    i_wg,
+    i_wb,
+    out,
+    grad,
+    o_w1,
+    o_w2,
+    o_k,
+    o_w3,
+    o_ng,
+    o_nb,
+    o_wg,
+    o_wb,
+    work,
+    zero,
+    in_sem,
+    out_sem,
+):
+    half = pb.shape[-1]
     extra = cap - FR
-    zero[...] = jnp.zeros(zero.shape, BF16)
     odd, first = where[0], where[1]
     live = jnp.where(odd == 0, first, 2 * FR - first)
-
-    def each(j, act):
+    arrays = ((a2w, a2r, out), (gw, gr, grad))
+
+    def source(j):
         pos = jnp.where(odd == 0, j, first + j)
         mine = jnp.where(odd == 0, pos < FR, pos >= FR)
         own = jnp.where(odd == 0, pos, pos - FR)
         far = jnp.where(odd == 0, pos - FR, pos - (FR - extra))
-        for i, (work, back, dst) in enumerate(((a2w, a2r, out), (gw, gr, grad))):
+        return mine, own, far
+
+    def fetch(j, carry):
+        mine, own, far = source(j)
+        for i, (near, back, _) in enumerate(arrays):
 
             @pl.when((j < live) & mine)
             def _():
-                act(pltpu.make_async_copy(work.at[own], dst.at[j], sem.at[i]))
+                pltpu.make_async_copy(near.at[own], work.at[i, j], in_sem.at[i, j]).start()
 
             @pl.when((j < live) & jnp.logical_not(mine))
             def _():
-                act(pltpu.make_async_copy(back.at[far], dst.at[j], sem.at[i]))
-
-            @pl.when(j >= live)
-            def _():
-                act(pltpu.make_async_copy(zero, dst.at[j], sem.at[i]))
-
-    def start(j, carry):
-        each(j, lambda cp: cp.start())
+                pltpu.make_async_copy(back.at[far], work.at[i, j], in_sem.at[i, j]).start()
+
         return carry
 
-    loop(0, cap, start)
-    pltpu.make_async_copy(out, out, sem.at[0]).wait()
-    pltpu.make_async_copy(grad, grad, sem.at[1]).wait()
-
-
-def place(dims, where, a2w, a2r, gw, gr):
+    loop(0, cap, fetch)
+    zero[...] = jnp.zeros(zero.shape, BF16)
+
+    def clear(j, carry):
+        for i, (_, _, dst) in enumerate(arrays):
+            pltpu.make_async_copy(zero, dst.at[j], out_sem.at[i]).start()
+        return carry
+
+    lax.fori_loop(live, cap, clear, 0)
+
+    def ship(j, carry):
+        for i, (near, _, dst) in enumerate(arrays):
+            pltpu.make_async_copy(near.at[0], work.at[i, j], in_sem.at[i, j]).wait()
+            pltpu.make_async_copy(work.at[i, j], dst.at[j], out_sem.at[i]).start()
+        return carry
+
+    lax.fori_loop(0, live, ship, 0)
+    o_ng[...] = i_ng[...]
+    o_nb[...] = i_nb[...]
+    o_wg[...] = i_wg[...]
+    o_wb[...] = i_wb[...]
+    for b in range(2):
+        for p in range(2):
+            cols = slice(p * 128, p * 128 + 128)
+            taps = pa[b, p, 0:2, :, half + 128 :].astype(F32).reshape(32, 128)
+            o_k[b, :, cols] = taps[0:27]
+            mid = pa[b, p, :, :, half : half + 128].astype(F32)
+            o_w2[b, :, cols] = mid.reshape(256, 128)
+            cols = slice(p * half, p * half + half)
+            o_w3[b, :, cols] = pa[b, p, :, :, 0:half].astype(F32).reshape(256, half)
+            o_w1[b, cols, :] = pb[b, p].astype(F32).reshape(256, half).T
+    pltpu.make_async_copy(out, out, out_sem.at[0]).wait()
+    pltpu.make_async_copy(grad, grad, out_sem.at[1]).wait()
+
+
+def place(dims, where, *parts):
     n_col, n_ta, cap, hh, ww, width, bot = dims
     sds = jax.ShapeDtypeStruct
     return pl.pallas_call(
-        functools.partial(place_kernel, dims),
-        out_shape=(sds((cap, hh, ww, width), BF16),) * 2,
-        in_specs=[SM] + [ANY] * 4,
-        out_specs=(ANY, ANY),
-        scratch_shapes=[pltpu.VMEM((hh, ww, width), BF16), pltpu.SemaphoreType.DMA((2,))],
+        functools.partial(place_kernel, cap),
+        out_shape=(sds((cap, hh, ww, width), BF16),) * 2
+        + (
+            sds((2, width, bot), F32),
+            sds((2, bot, bot), F32),
+            sds((2, 27, bot), F32),
+            sds((2, bot, width), F32),
+            sds((2, 2, bot), F32),
+            sds((2, 2, bot), F32),
+            sds((2, width), F32),
+            sds((2, width), F32),
+        ),
+        in_specs=[SM] + [ANY] * 4 + [VM] * 6,
+        out_specs=(ANY, ANY) + (VM,) * 8,
+        scratch_shapes=[
+            pltpu.VMEM((2, cap, hh, ww, width), BF16),
+            pltpu.VMEM((hh, ww, width), BF16),
+            pltpu.SemaphoreType.DMA((2, cap)),
+            pltpu.SemaphoreType.DMA((2,)),
+        ],
+        compiler_params=pltpu.CompilerParams(vmem_limit_bytes=64_000_000),
         name="place",
-    )(where, a2w, a2r, gw, gr)
+    )(where, *parts)
 
 
 def body(
@@ -874,7 +1109,7 @@
     begins = jnp.any(starts[None, :] == ids[:, None], axis=1) | (ids >= n_ta * FR)
     ok = jnp.logical_not(begins).astype(F32)
     okmask = jnp.stack([ok[:-1], ok[1:]])
-    (a2w, a2r, gw, gr, g_w1t, g_w2, g_w3, g_k, g_ng, g_nb, g_wg, g_wb) = run_main(
+    parts = run_main(
         dims,
         held,
         okmask,
@@ -890,20 +1125,7 @@
         wide_bias,
     )
     where = jnp.stack([odd, held[col, ta - odd]]).astype(jnp.int32)
-    out, grad = place(dims, where, a2w, a2r, gw, gr)
-    g_w1t, g_w2, g_w3, g_k = lax.psum((g_w1t, g_w2, g_w3, g_k), ("col", "ta"))
-    return (
-        out,
-        grad,
-        jnp.swapaxes(g_w1t, 1, 2),
-        g_w2,
-        g_k,
-        g_w3,
-        g_ng,
-        g_nb,
-        g_wg,
-        g_wb,
-    )
+    return place(dims, where, *parts)
 
 
 def solution(mesh):

time: 860 us -> 267 us (0.31)
  the two profiles are of different devices: /device:TPU:31 before, /device:TPU:0 now
where the time goes in v2:
time: 267 us
  Pallas kernels  259 us (97%)
  local copies, waits for them, and re-layouts  4.22 us (2%)
  other arithmetic  2.97 us (1%)
    pallas_call x1, Pallas kernels, run_main(): pl.pallas_call(functools.partial(main_kernel, dims), out_shape=outs, in_s...  243 us
    pallas_call x1, Pallas kernels, place(): pl.pallas_call(functools.partial(place_kernel, cap), out_shape=(sds((cap,...  16.5 us

profile of v2, /device:TPU:0, one launch (start us, length us, event | category | flops | bytes accessed | tf_op | source)
XLA Modules:
  0.0 267.1 jit_solution(17389070185663087500)
XLA Ops:
  0.7 1.3 dynamic_slice.7
  1.9 1.3 pad_add_fusion.where
  3.2 0.8 bitcast_select_fusion
  4.0 0.1 select_reduce_fusion
  4.1 0.2 compare_reduce_fusion
  4.3 0.1 slice_bitcast_fusion.1
  4.4 0.6 pad_maximum_fusion.okmask
  5.0 1.4 copy.24.taps
  6.3 242.7 %blocks.1 = (bf16[12,14,14,1024]{3,2,1,0:T(8,128)(2,1)}, bf16[9,14,14,1024]{3,2,1,0:T(8,128)(2,1)}, bf16[12,14,14,1024]{3,2,1,0:T(8,128)(2,1)}, bf16[9,14,14,102...) custom-call(s32[4,8]{1,0:T(4,128)} %held.1, ...), custom_call_target="tpu_custom_call" | custom-call | tf_op jit(solution)/shard_map/blocks/pallas_call | solution.py:952
  249.0 16.5 %place.1 = (bf16[21,14,14,1024]{3,2,1,0:T(8,128)(2,1)}, bf16[21,14,14,1024]{3,2,1,0:T(8,128)(2,1)}, f32[2,1024,256]{2,1,0:T(8,128)}, f32[2,256,256]{2,1,0:T(8,12...) custom-call(s32[2]{0:T(128)} %pad_add_fusion.where, ...), custom_call_target="tpu_custom_call" | custom-call | tf_op jit(solution)/shard_map/place/pallas_call | solution.py:1058
  265.6 1.5 copy.25
  (2 shorter events, 0.0 us)

commit v3 on v2

--- a/solution.py
+++ b/solution.py
@@ -109,6 +109,7 @@
     n_col, n_ta, cap, hh, ww, width, bot = dims
     n_dev = n_col * n_ta
     extra = cap - FR
+    N1, N3, NA, NZ2, NZ1, NW, NM = (3, 2, 2, 1, 3, 4, 2) if n_dev <= 64 else (1,) * 7
     wp = 16
     rf = hh * wp
     stride = (hh + 2) * wp
@@ -262,15 +263,15 @@
             total = jnp.sum(exchange("all", total, between), axis=0)
         return total[0:1], total[1:2]
 
-    def rows(f):
-        return pl.ds(pl.multiple_of(f * rf, rf), rf)
-
-    def ld_h(f):
-        return jnp.concatenate([hbuf[0, rows(f)], hbuf[1, rows(f)]], axis=1)
-
-    def st_h(f, values):
-        hbuf[0, rows(f)] = values[:, :128]
-        hbuf[1, rows(f)] = values[:, 128:]
+    def rows(f, n=1):
+        return pl.ds(pl.multiple_of(f * (n * rf), rf), n * rf)
+
+    def ld_h(f, n=1):
+        return jnp.concatenate([hbuf[0, rows(f, n)], hbuf[1, rows(f, n)]], axis=1)
+
+    def st_h(f, values, n=1):
+        hbuf[0, rows(f, n)] = values[:, :128]
+        hbuf[1, rows(f, n)] = values[:, 128:]
 
     def conv_rows(slot):
         return pl.ds(pl.multiple_of(lead + slot * stride + wp, 8), rf)
@@ -324,7 +325,7 @@
         loop(0, 2, half)
 
     def load_taps(b):
-        k = taps[b].astype(F32)
+        k = taps[...].astype(F32)[:, b]
         prm[0, 0:27] = k[:, :128]
         prm[1, 0:27] = k[:, 128:]
 
@@ -350,11 +351,11 @@
     def chunk(c):
         return pl.ds(c * 256, 256)
 
-    def flat(ref, f, c):
-        return ref[f, :, :, chunk(c)].reshape(rf, 256)
-
-    def put(ref, f, c, values):
-        ref[f, :, :, chunk(c)] = values.reshape(hh, wp, 256)
+    def flat(ref, f, c, n=1):
+        return ref[pl.ds(f * n, n), :, :, chunk(c)].reshape(n * rf, 256)
+
+    def put(ref, f, c, values, n=1):
+        ref[pl.ds(f * n, n), :, :, chunk(c)] = values.reshape(n, hh, wp, 256)
 
     nz = n_ta // 2
     zpos = lax.div(ta, 2)
@@ -494,12 +495,12 @@
         sacc[0:wp, 0:bot] = jnp.zeros((wp, bot), F32)
 
         def to_h1(f, carry):
-            h1 = dot_nn(src[f].reshape(rf, width), w1[b])
-            st_h(f, h1)
+            h1 = dot_nn(src[pl.ds(f * N1, N1)].reshape(N1 * rf, width), w1[b])
+            st_h(f, h1, N1)
             sacc[0:wp, 0:bot] += rowsum(h1)
             return carry
 
-        loop(0, FR, to_h1)
+        loop(0, FR // N1, to_h1)
         mean_l = live_total(sacc[0:wp, 0:bot]) * (1.0 / n_local)
         return mean_l, local_m2(mean_l)
 
@@ -571,14 +572,14 @@
         sacc[...] = jnp.zeros(sacc.shape, F32)
 
         def h3_stats(f, carry):
-            left = u2b[b, rows(f)]
+            left = u2b[b, rows(f, N3)]
             for c in range(chunks):
                 h3 = dot_nn(left, w3[b, :, chunk(c)]) - pivot[:, c * 256 : c * 256 + 256]
                 sacc[0:wp, chunk(c)] += rowsum(h3)
                 sacc[wp : 2 * wp, chunk(c)] += rowsum(h3 * h3)
             return carry
 
-        loop(0, FR, h3_stats)
+        loop(0, FR // N3, h3_stats)
         s1 = live_total(sacc[0:wp]) * (1.0 / n_local)
         s2 = live_total(sacc[wp : 2 * wp])
         mean3[b], inv3[b] = moments(pivot + s1, s2 - n_local * s1 * s1, True, None)
@@ -594,15 +595,15 @@
     sc, sh = g3 * inv3[0], b3 - mean3[0] * g3 * inv3[0]
 
     def to_a1(f, carry):
-        left = u2b[0, rows(f)]
+        left = u2b[0, rows(f, NA)]
         for c in range(chunks):
             s = slice(c * 256, c * 256 + 256)
             h3 = dot_nn(left, w3[0, :, chunk(c)])
-            pre = flat(a0, f, c).astype(F32) + (h3 * sc[:, s] + sh[:, s])
-            put(a1, f, c, silu(pre).astype(BF16))
+            pre = flat(a0, f, c, NA).astype(F32) + (h3 * sc[:, s] + sh[:, s])
+            put(a1, f, c, silu(pre).astype(BF16), NA)
         return carry
 
-    loop(0, FR, to_a1)
+    loop(0, FR // NA, to_a1)
 
     def none():
         pass
@@ -673,24 +674,24 @@
         wacc[...] = jnp.zeros((bot, width), F32)
 
         def to_z2(f, carry):
-            left = u2b[b, rows(f)]
+            left = u2b[b, rows(f, NZ2)]
             for c in range(chunks):
                 s = slice(c * 256, c * 256 + 256)
                 h3 = dot_nn(left, w3[b, :, chunk(c)])
-                dh3 = flat(pbuf, f, c).astype(F32) * k3[:, s] - h3 * ch[:, s] + cc[:, s]
+                dh3 = flat(pbuf, f, c, NZ2).astype(F32) * k3[:, s] - h3 * ch[:, s] + cc[:, s]
                 tile[:, chunk(c)] = dh3.astype(BF16)
             du2 = dot_nt(tile[...], w3[b])
             for c in range(chunks):
                 wacc[:, chunk(c)] += dot_tn(left, tile[:, chunk(c)])
-            xhat = x2b[b, rows(f)].astype(F32)
+            xhat = x2b[b, rows(f, NZ2)].astype(F32)
             _, slope = silu_and_slope(xhat * g2 + b2)
             z = du2 * slope
-            st_h(f, z)
+            st_h(f, z, NZ2)
             sacc[0:wp, 0:bot] += rowsum(z)
             sacc[wp : 2 * wp, 0:bot] += rowsum(z * xhat)
             return carry
 
-        loop(0, FR, to_z2)
+        loop(0, FR // NZ2, to_z2)
         s0, s1 = sums(
             live_total(sacc[0:wp, 0:bot]), live_total(sacc[wp : 2 * wp, 0:bot]), False, windows[2]
         )
@@ -724,18 +725,18 @@
         w2acc[...] = jnp.zeros((bot, bot), F32)
 
         def to_z1(f, carry):
-            dh2 = ld_h(f).astype(BF16)
-            xhat = x1b[b, rows(f)].astype(F32)
+            dh2 = ld_h(f, NZ1).astype(BF16)
+            xhat = x1b[b, rows(f, NZ1)].astype(F32)
             act, slope = silu_and_slope(xhat * g1 + b1)
             u1 = masked(act).astype(BF16)
             w2acc[...] += dot_tn(u1, dh2)
             z = dot_nt(dh2, w2[b]) * slope
-            st_h(f, z)
+            st_h(f, z, NZ1)
             sacc[0:wp, 0:bot] += rowsum(z)
             sacc[wp : 2 * wp, 0:bot] += rowsum(z * xhat)
             return carry
 
-        loop(0, FR, to_z1)
+        loop(0, FR // NZ1, to_z1)
         def tap_grads():
             kacc[...] = jnp.zeros(kacc.shape, F32)
 
@@ -795,12 +796,12 @@
             wacc[...] = jnp.zeros((bot, width), F32)
 
             def to_w1(f, carry):
-                left = x1b[b, rows(f)]
+                left = x1b[b, rows(f, NW)]
                 for c in range(chunks):
-                    wacc[:, chunk(c)] += dot_tn(left, flat(act_src, f, c))
+                    wacc[:, chunk(c)] += dot_tn(left, flat(act_src, f, c, NW))
                 return carry
 
-            loop(0, FR, to_w1)
+            loop(0, FR // NW, to_w1)
             pack_b()
             gen = package(pb_bufs, pb_sem, o_pb.at[b])
             next(gen)
@@ -817,37 +818,45 @@
     sacc[...] = jnp.zeros(sacc.shape, F32)
 
     def middle(f, carry):
-        left = u2b[0, rows(f)]
-        dh1 = x1b[1, rows(f)]
+        left = u2b[0, rows(f, NM)]
+        dh1 = x1b[1, rows(f, NM)]
         for c in range(chunks):
             s = slice(c * 256, c * 256 + 256)
-            grad = dot_nt(dh1, w1[1, chunk(c), :]) + flat(pbuf, f, c).astype(F32)
+            grad = dot_nt(dh1, w1[1, chunk(c), :]) + flat(pbuf, f, c, NM).astype(F32)
             h3 = dot_nn(left, w3[0, :, chunk(c)])
             xhat = h3 * inv3[0][:, s] - nxhat[:, s]
-            pre = flat(a0, f, c).astype(F32) + (xhat * g3[:, s] + b3[:, s])
+            pre = flat(a0, f, c, NM).astype(F32) + (xhat * g3[:, s] + b3[:, s])
             _, slope = silu_and_slope(pre)
             grad = grad * slope
-            put(pbuf, f, c, grad.astype(BF16))
+            put(pbuf, f, c, grad.astype(BF16), NM)
             sacc[0:wp, chunk(c)] += rowsum(grad)
             sacc[wp : 2 * wp, chunk(c)] += rowsum(grad * xhat)
         return carry
 
-    loop(0, FR, middle)
+    advance(gen_a)
+    loop(0, FR // NM, middle)
     sum_p, sum_px = live_total(sacc[0:wp]), live_total(sacc[wp : 2 * wp])
-    gens = [gen_a]
+    gens = []
 
     def window0():
+        gens.append(w1_grad())
         advance(gen_a)
-        gens.append(w1_grad())
 
     def window1():
-        advance(*gens)
+        pass
+
+    def window2():
+        advance(gen_a, gens[0])
+
+    def window3():
+        advance(gen_a, gens[0])
 
     def window4():
-        for gen in gens:
-            finish(gen)
-
-    w1_last, last_a = block_backward(0, a0, [window0, window1, window1, window1, window4])
+        advance(gens[0])
+        finish(gen_a)
+
+    w1_last, last_a = block_backward(0, a0, [window0, window1, window2, window3, window4])
+    finish(gens[0])
     last_b = w1_last()
     advance(last_a)
 
@@ -1042,7 +1051,7 @@
         for p in range(2):
             cols = slice(p * 128, p * 128 + 128)
             taps = pa[b, p, 0:2, :, half + 128 :].astype(F32).reshape(32, 128)
-            o_k[b, :, cols] = taps[0:27]
+            o_k[:, b, cols] = taps[0:27]
             mid = pa[b, p, :, :, half : half + 128].astype(F32)
             o_w2[b, :, cols] = mid.reshape(256, 128)
             cols = slice(p * half, p * half + half)
@@ -1061,7 +1070,7 @@
         + (
             sds((2, width, bot), F32),
             sds((2, bot, bot), F32),
-            sds((2, 27, bot), F32),
+            sds((27, 2, bot), F32),
             sds((2, bot, width), F32),
             sds((2, 2, bot), F32),
             sds((2, 2, bot), F32),
@@ -1118,14 +1127,15 @@
         w_reduce,
         w_mid,
         w_expand,
-        depth_kernel,
+        jnp.swapaxes(depth_kernel, 0, 1),
         narrow_gain,
         narrow_bias,
         wide_gain,
         wide_bias,
     )
     where = jnp.stack([odd, held[col, ta - odd]]).astype(jnp.int32)
-    return place(dims, where, *parts)
+    outs = place(dims, where, *parts)
+    return outs[:4] + (jnp.swapaxes(outs[4], 0, 1),) + outs[5:]
 
 
 def solution(mesh):

time: 267 us -> 246 us (0.921)
  Pallas kernels: 259 us -> 241 us
  local copies, waits for them, and re-layouts: 4.22 us -> 1.35 us
    pallas_call x1, Pallas kernels: 243 us -> 224 us  [run_main(): pl.pallas_call(functools.partial(main_kernel, dims), out_shape=outs, in_s...]
where the time goes in v3:
time: 246 us
  Pallas kernels  241 us (98%)
  other arithmetic  2.96 us (1%)
    pallas_call x1, Pallas kernels, run_main(): pl.pallas_call(functools.partial(main_kernel, dims), out_shape=outs, in_s...  224 us
    pallas_call x1, Pallas kernels, place(): pl.pallas_call(functools.partial(place_kernel, cap), out_shape=(sds((cap,...  17.3 us

profile of v3, /device:TPU:0, one launch (start us, length us, event | category | flops | bytes accessed | tf_op | source)
XLA Modules:
  0.0 246.2 jit_solution(14096706779536184168)
XLA Ops:
  0.7 1.3 dynamic_slice.7
  1.9 1.3 pad_add_fusion.where
  3.2 0.8 bitcast_select_fusion
  4.0 0.1 select_reduce_fusion
  4.1 0.2 compare_reduce_fusion
  4.3 0.1 slice_bitcast_fusion.1
  4.4 0.6 pad_maximum_fusion.okmask
  5.0 223.7 %blocks.1 = (bf16[12,14,14,1024]{3,2,1,0:T(8,128)(2,1)}, bf16[9,14,14,1024]{3,2,1,0:T(8,128)(2,1)}, bf16[12,14,14,1024]{3,2,1,0:T(8,128)(2,1)}, bf16[9,14,14,102...) custom-call(s32[4,8]{1,0:T(4,128)} %held.1, ...), custom_call_target="tpu_custom_call" | custom-call | tf_op jit(solution)/shard_map/blocks/pallas_call | solution.py:961
  228.7 17.3 %place.1 = (bf16[21,14,14,1024]{3,2,1,0:T(8,128)(2,1)}, bf16[21,14,14,1024]{3,2,1,0:T(8,128)(2,1)}, f32[2,1024,256]{2,1,0:T(8,128)}, f32[2,256,256]{2,1,0:T(8,12...) custom-call(s32[2]{0:T(128)} %pad_add_fusion.where, ...), custom_call_target="tpu_custom_call" | custom-call | tf_op jit(solution)/shard_map/place/pallas_call | solution.py:1067
  (2 shorter events, 0.0 us)

commit v4 on v3

--- a/solution.py
+++ b/solution.py
@@ -109,7 +109,7 @@
     n_col, n_ta, cap, hh, ww, width, bot = dims
     n_dev = n_col * n_ta
     extra = cap - FR
-    N1, N3, NA, NZ2, NZ1, NW, NM = (3, 2, 2, 1, 3, 4, 2) if n_dev <= 64 else (1,) * 7
+    N1, N3, NA, NZ2, NZ1, NW, NM = (3, 2, 2, 2, 3, 4, 2) if n_dev <= 64 else (1,) * 7
     wp = 16
     rf = hh * wp
     stride = (hh + 2) * wp
@@ -926,7 +926,7 @@
         vm((FR, hh, 16, width), BF16),
         vm((FR, hh, 16, width), BF16),
         vm((FR, hh, 16, width), BF16),
-        vm((rf, width), BF16),
+        vm(((2 if n_dev <= 64 else 1) * rf, width), BF16),
         vm((2, hh, ww, width), BF16),
         vm((2, FR * rf, bot), BF16),
         vm((2, FR * rf, 128), F32),
@@ -973,7 +973,7 @@
 
 def place_kernel(
     cap,
-    where,
+    held,
     a2w,
     a2r,
     gw,
@@ -1001,7 +1001,9 @@
 ):
     half = pb.shape[-1]
     extra = cap - FR
-    odd, first = where[0], where[1]
+    col, ta = lax.axis_index("col"), lax.axis_index("ta")
+    odd = lax.rem(ta, 2)
+    first = held[col, ta - odd]
     live = jnp.where(odd == 0, first, 2 * FR - first)
     arrays = ((a2w, a2r, out), (gw, gr, grad))
 
@@ -1061,7 +1063,7 @@
     pltpu.make_async_copy(grad, grad, out_sem.at[1]).wait()
 
 
-def place(dims, where, *parts):
+def place(dims, held, *parts):
     n_col, n_ta, cap, hh, ww, width, bot = dims
     sds = jax.ShapeDtypeStruct
     return pl.pallas_call(
@@ -1087,7 +1089,7 @@
         ],
         compiler_params=pltpu.CompilerParams(vmem_limit_bytes=64_000_000),
         name="place",
-    )(where, *parts)
+    )(held, *parts)
 
 
 def body(
@@ -1109,7 +1111,6 @@
     cap, hh, ww, width = frames.shape
     dims = (n_col, n_ta, cap, hh, ww, width, w_mid.shape[1])
     col, ta = lax.axis_index("col"), lax.axis_index("ta")
-    odd = lax.rem(ta, 2)
     lengths = 8 // lax.dynamic_index_in_dim(clip_stride, col, 0, keepdims=False)
     clips = lengths.shape[0]
     before = jnp.arange(clips)[:, None] < jnp.arange(clips)[None, :]
@@ -1133,8 +1134,7 @@
         wide_gain,
         wide_bias,
     )
-    where = jnp.stack([odd, held[col, ta - odd]]).astype(jnp.int32)
-    outs = place(dims, where, *parts)
+    outs = place(dims, held, *parts)
     return outs[:4] + (jnp.swapaxes(outs[4], 0, 1),) + outs[5:]
 
 

time: 246 us -> 241 us (0.980)
  the two profiles are of different devices: /device:TPU:0 before, /device:TPU:10 now
where the time goes in v4:
time: 241 us; the launch traced here: 239 us
  Pallas kernels  236 us (98%)
    pallas_call x1, Pallas kernels, run_main(): pl.pallas_call(functools.partial(main_kernel, dims), out_shape=outs, in_s...  219 us
    pallas_call x1, Pallas kernels, place(): pl.pallas_call(functools.partial(place_kernel, cap), out_shape=(sds((cap,...  17.3 us

profile of v4, /device:TPU:10, one launch (start us, length us, event | category | flops | bytes accessed | tf_op | source)
XLA Modules:
  0.0 238.6 jit_solution(8062370656452789553)
XLA Ops:
  0.6 0.8 bitcast_select_fusion
  1.5 0.1 select_reduce_fusion
  1.6 0.2 compare_reduce_fusion
  1.8 0.1 slice_bitcast_fusion.1
  1.8 0.6 pad_maximum_fusion.okmask
  2.4 218.7 %blocks.1 = (bf16[12,14,14,1024]{3,2,1,0:T(8,128)(2,1)}, bf16[9,14,14,1024]{3,2,1,0:T(8,128)(2,1)}, bf16[12,14,14,1024]{3,2,1,0:T(8,128)(2,1)}, bf16[9,14,14,102...) custom-call(s32[4,8]{1,0:T(4,128)} %held.3, ...), custom_call_target="tpu_custom_call" | custom-call | tf_op jit(solution)/shard_map/blocks/pallas_call | solution.py:961
  221.1 17.3 %place.1 = (bf16[21,14,14,1024]{3,2,1,0:T(8,128)(2,1)}, bf16[21,14,14,1024]{3,2,1,0:T(8,128)(2,1)}, f32[2,1024,256]{2,1,0:T(8,128)}, f32[2,256,256]{2,1,0:T(8,12...) custom-call(s32[4,8]{1,0:T(4,128)} %held.3, ...), custom_call_target="tpu_custom_call" | custom-call | tf_op jit(solution)/shard_map/place/pallas_call | solution.py:1069
  (2 shorter events, 0.0 us)

commit v5 on v4

--- a/solution.py
+++ b/solution.py
@@ -857,6 +857,7 @@
 
     w1_last, last_a = block_backward(0, a0, [window0, window1, window2, window3, window4])
     finish(gens[0])
+    advance(last_a)
     last_b = w1_last()
     advance(last_a)
 
@@ -873,10 +874,12 @@
         out_copy(f, gw).start()
         return carry
 
-    half_way = FR // 2
-    loop(0, half_way, last)
-    advance(last_a, last_b)
-    loop(half_way, FR, last)
+    third = FR // 3
+    loop(0, third, last)
+    advance(last_b, last_a)
+    loop(third, 2 * third, last)
+    advance(last_b, last_a)
+    loop(2 * third, FR, last)
     out_copy(FR - 2, gw).wait()
     out_copy(FR - 1, gw).wait()
     ret_g = swap_out(gw, gr, 1)

time: 241 us -> 240 us (level)
  the two profiles are of different devices: /device:TPU:10 before, /device:TPU:0 now
where the time goes in v5:
time: 240 us
  Pallas kernels  237 us (99%)
    pallas_call x1, Pallas kernels, run_main(): pl.pallas_call(functools.partial(main_kernel, dims), out_shape=outs, in_s...  221 us
    pallas_call x1, Pallas kernels, place(): pl.pallas_call(functools.partial(place_kernel, cap), out_shape=(sds((cap,...  16.7 us

profile of v5, /device:TPU:0, one launch (start us, length us, event | category | flops | bytes accessed | tf_op | source)
XLA Modules:
  0.0 240.0 jit_solution(6145411925753055294)
XLA Ops:
  0.6 0.8 bitcast_select_fusion
  1.5 0.1 select_reduce_fusion
  1.6 0.2 compare_reduce_fusion
  1.8 0.1 slice_bitcast_fusion.1
  1.8 0.6 pad_maximum_fusion.okmask
  2.4 220.7 %blocks.1 = (bf16[12,14,14,1024]{3,2,1,0:T(8,128)(2,1)}, bf16[9,14,14,1024]{3,2,1,0:T(8,128)(2,1)}, bf16[12,14,14,1024]{3,2,1,0:T(8,128)(2,1)}, bf16[9,14,14,102...) custom-call(s32[4,8]{1,0:T(4,128)} %held.3, ...), custom_call_target="tpu_custom_call" | custom-call | tf_op jit(solution)/shard_map/blocks/pallas_call | solution.py:964
  223.1 16.7 %place.1 = (bf16[21,14,14,1024]{3,2,1,0:T(8,128)(2,1)}, bf16[21,14,14,1024]{3,2,1,0:T(8,128)(2,1)}, f32[2,1024,256]{2,1,0:T(8,128)}, f32[2,256,256]{2,1,0:T(8,12...) custom-call(s32[4,8]{1,0:T(4,128)} %held.3, ...), custom_call_target="tpu_custom_call" | custom-call | tf_op jit(solution)/shard_map/place/pallas_call | solution.py:1072
  (2 shorter events, 0.0 us)
